TPU v7x, 256 devices: a whole 4x4x8 slice. The times are simulated.
256 devices in a mesh: tm: 16 (over x_hi, y, core), chan: 16 (over z, x_lo).
Axes of the slice: x: 4 (x_hi: 2, x_lo: 2; x = x_hi * 2 + x_lo), y: 4, z: 8, core: 2. Of those that a mesh axis runs over, the one named last changes fastest.
Arguments:
- voltages: bfloat16 [2, 512, 524288], P(None, 'chan', 'tm'), may hold values from -6 to 6
- filter_taps: float32 [16, 1024], replicated, may hold values from -1.5 to 1.5
- slot_station: int32 [256], replicated, may hold values from 0 to 255, each once
- pair_blocks: int32 [10, 2], replicated, may hold values from 0 to 3, as said below
Outputs:
- visibilities: float32 [1024, 10, 2, 128, 128], P(('chan', 'tm'))
Inputs may be any that keep to these rules, and one draw needn't show every extreme that they name: `slot_station`: each station stands in exactly one slot. `pair_blocks`: every pair (row tile, column tile) of tiles of 128 inputs with row tile >= column tile stands in exactly one row, row tile first.
All inputs are finite; a program needn't handle non-finite values.
Results may differ from a plain program's by a relative error of at most 0.0041.
Values may be sent and summed in bfloat16 or wider, within the bound.
No kernel may reach another device: no remote copies, remote signals or barrier semaphores. Data moves between devices by JAX's collectives and lax.ppermute only.
A program may use at most 192 MiB of HBM per device.

v0:
```python
import math

import jax
import jax.numpy as jnp
from jax import lax
from jax.sharding import PartitionSpec as P

TILE = 128


def from_behind(value, axis, steps):
    count = lax.axis_size(axis)
    first, last = (max(0, -steps), min(count, count - steps))
    return lax.ppermute(value, axis, [(source, source + steps) for source in range(first, last)])


def dft_table(channels):
    indices = jnp.arange(channels, dtype=jnp.int32)
    products = indices[:, None] * indices[None, :] % channels
    angles = products.astype(jnp.float32) * (2.0 * math.pi / channels)
    cosine = jnp.cos(angles) / math.sqrt(channels)
    sine_part = jnp.sin(angles) / math.sqrt(channels)
    upper_half = jnp.concatenate([cosine, -sine_part], 1)
    lower_half = jnp.concatenate([sine_part, cosine], 1)
    return jnp.concatenate([upper_half, lower_half], 0).astype(jnp.bfloat16)


def slot_order(slot_station, inputs):
    stations = slot_station.shape[0]
    positions = jnp.arange(stations, dtype=jnp.int32)
    inverse = jnp.zeros((stations,), jnp.int32).at[slot_station].set(positions)
    indices = jnp.arange(inputs, dtype=jnp.int32)
    return 2 * inverse[indices // 2] + indices % 2


def combine_parts(gram_part, tile_size):
    real_part = gram_part[:tile_size, :tile_size] + gram_part[tile_size:, tile_size:]
    imag_part = gram_part[tile_size:, :tile_size] - gram_part[:tile_size, tile_size:]
    return jnp.stack([real_part, imag_part])


def contract_time(left_cols, right_cols):
    return lax.dot_general(
        left_cols, right_cols, (((0,), (0,)), ((), ())), preferred_element_type=jnp.float32
    )


def local(voltages, filter_taps, slot_station, pair_blocks):
    tap_count, channels = filter_taps.shape
    local_inputs = voltages.shape[1]
    frame_count = voltages.shape[2] // channels
    tail_part = voltages[:, :, voltages.shape[2] - (tap_count - 1) * channels :]
    earlier = from_behind(tail_part, "tm", 1)
    extended = jnp.concatenate([earlier, voltages], 2).reshape(
        2, local_inputs, frame_count + tap_count - 1, channels
    )
    summed = jnp.zeros((2, local_inputs, frame_count, channels), jnp.float32)
    for tap_index in range(tap_count):
        summed = summed + filter_taps[tap_index] * extended[
            :, :, tap_index : tap_index + frame_count, :
        ].astype(jnp.float32)
    filtered = jnp.swapaxes(summed.astype(jnp.bfloat16), 1, 2)
    joined = jnp.concatenate([filtered[0], filtered[1]], -1).reshape(
        frame_count * local_inputs, 2 * channels
    )
    spectra = lax.dot_general(
        dft_table(channels), joined, (((0,), (1,)), ((), ())), preferred_element_type=jnp.float32
    ).astype(jnp.bfloat16)
    n_chan = lax.axis_size("chan")
    n_time = lax.axis_size("tm")
    chan_count = channels // (n_chan * n_time)
    split_view = spectra.reshape(2, n_chan, n_time, chan_count, frame_count * local_inputs)
    by_owner = lax.all_to_all(split_view, "chan", split_axis=1, concat_axis=1, tiled=True)
    received = lax.all_to_all(by_owner, "tm", split_axis=2, concat_axis=2, tiled=True)
    received = received.reshape(2, n_chan, n_time, chan_count, frame_count, local_inputs)
    all_inputs = n_chan * local_inputs
    turned = jnp.transpose(received, (3, 0, 2, 4, 1, 5)).reshape(
        chan_count, 2, n_time * frame_count, all_inputs
    )
    input_slot = slot_order(slot_station, all_inputs)
    per_channel = jnp.take(turned, input_slot, axis=3)
    norm_scale = 1.0 / (n_time * frame_count)
    tile_size = TILE

    def one_channel(channel_data):

        def one_block(pair):
            row_cols = lax.dynamic_slice_in_dim(channel_data, pair[0] * tile_size, tile_size, 2)
            col_cols = lax.dynamic_slice_in_dim(channel_data, pair[1] * tile_size, tile_size, 2)
            left_cols = jnp.concatenate([row_cols[0], row_cols[1]], 1)
            right_cols = jnp.concatenate([col_cols[0], col_cols[1]], 1)
            return combine_parts(contract_time(left_cols, right_cols), tile_size) * norm_scale

        return jax.vmap(one_block)(pair_blocks)

    return jax.vmap(one_channel)(per_channel)


def solution(mesh):
    in_specs = (P(None, "chan", "tm"), P(), P(), P())
    out_specs = P(("chan", "tm"), None, None, None, None)
    return jax.shard_map(local, mesh=mesh, in_specs=in_specs, out_specs=out_specs, check_vma=False)
```

profile of v0, /device:TPU:29, one launch (start us, length us, event | category | flops | bytes accessed | tf_op | source)
XLA Modules:
  0.0 572.5 jit_solution(6173178858394850385)
XLA Ops:
  4.6 15.8 %fusion.31 = bf16[1024,1024]{1,0:T(8,128)(2,1)S(1)} fusion(), kind=kLoop, calls=%fused_computation.50 | loop fusion | flops 16777216 | bytes 2097152 | tf_op jit(solution)/shard_map/convert.2
  20.4 17.9 %negate_convert_fusion = (bf16[1024,1024]{1,0:T(8,128)(2,1)}, bf16[1024,1024]{1,0:T(8,128)(2,1)}) fusion(), kind=kLoop, calls=%fused_computation.42 | loop fusion | flops 19922944 | bytes 4194304 | tf_op jit(solution)/shard_map/convert.5
  38.3 3.0 pad_maximum_fusion
  41.4 8.9 %reshape.119 = bf16[2,32,47,1024]{3,2,1,0:T(8,128)(2,1)} reshape(bf16[2,32,48128]{2,1,0:T(8,128)(2,1)} %pad_maximum_fusion) | data formatting | bytes 12320768 | tf_op jit(solution)/shard_map/reshape | solution.py:54
  50.2 43.4 %fusion.25 = bf16[2,32,32,1024]{3,1,2,0:T(8,128)(2,1)S(1)} fusion(bf16[2,32,47,1024]{3,2,1,0:T(8,128)(2,1)} %reshape.119, f32[1024]{0:T(1024)S(1)} %bitcast.84, f32[1024]{0:T(1024)S(1)} %bitcast.85, f32[1024]{0:T(1024)S(1)} %bitcast.71, f32[1024]{0:T(1024)S(1)} %bitcast.72, f32[1024]{0:T(1024)S(1)} %bitcast.73, f32[1024]{0:T(1024)S(1)} %bitcast.74, ...), kind=kLoop, calls=%fused_computation.48 | loop fusion | flops 100663296 | bytes 71368704 | tf_op jit(solution)/shard_map/transpose | solution.py:62
  94.1 2.5 copy.27
  96.6 2.5 copy.26
  99.1 21.2 %fusion.26 = bf16[2048,1024]{1,0:T(8,128)(2,1)} fusion(bf16[1024,1024]{1,0:T(8,128)(2,1)} %bitcast.68, bf16[1024,1024]{1,0:T(8,128)(2,1)} %bitcast.69, bf16[1024,1024]{1,0:T(8,128)(2,1)} %get-tuple-element.88, bf16[1024,1024]{1,0:T(8,128)(2,1)S(1)} %fusion.31, bf16[1024,1024]{1,0:T(8,128)(2,1)} %get-tuple-element.87), kind=kOutput, calls=%fused_computation.49 | convolution fusion | flops 8633974784 | bytes 14680064 | tf_op jit(solution)/shard_map/dot_general | solution.py:66
  120.3 17.2 %reshape.120 = bf16[2,16,16,4,1024]{4,3,2,1,0:T(4,128)(2,1)} reshape(bf16[2048,1024]{1,0:T(8,128)(2,1)} %fusion.26) | data formatting | bytes 8388608 | tf_op jit(solution)/shard_map/reshape | solution.py:72
  137.5 4.0 copy.28
  141.4 102.6 %all_to_all.10 = bf16[2,16,16,4,1024]{4,2,3,0,1:T(8,128)(2,1)S(1)} all-to-all(bf16[2,16,16,4,1024]{4,2,3,0,1:T(8,128)(2,1)S(1)} %copy.28), channel_id=1, replica_groups=mesh['tm'=16,'chan'=16] {'chan'}, dimensions={1} | all-to-all | bytes 8388608 | tf_op jit(solution)/shard_map/all_to_all | solution.py:73
  244.1 5.2 copy.29
  249.3 11.8 %all-to-all-start.1 = ((bf16[2,16,16,4,1024]{4,3,1,0,2:T(4,128)(2,1)}), bf16[2,16,16,4,1024]{4,3,1,0,2:T(4,128)(2,1)}, u32[]{:S(2)}, u32[]{:S(2)}) async-start(bf16[2,16,16,4,1024]{4,3,1,0,2:T(4,128)(2,1)} %copy.29), calls=%async_computation.1 | async-start | bytes 8388608 | tf_op jit(solution)/shard_map/all_to_all | solution.py:74
  262.6 3.5 gather_fusion
  266.2 56.3 %all-to-all-done.1 = bf16[2,16,16,4,1024]{4,3,1,0,2:T(4,128)(2,1)} async-done(((bf16[2,16,16,4,1024]{4,3,1,0,2:T(4,128)(2,1)}), bf16[2,16,16,4,1024]{4,3,1,0,2:T(4,128)(2,1)}, u32[]{:S(2)}, u32[]{:S(2)}) %all-to-all-start.1) | async-done | bytes 4194336 | tf_op jit(solution)/shard_map/all_to_all | solution.py:74
  322.5 7.6 %copy.30 = bf16[2,16,16,4,1024]{4,2,3,1,0:T(8,128)(2,1)} copy(bf16[2,16,16,4,1024]{4,3,1,0,2:T(4,128)(2,1)} %all-to-all-done.1) | data formatting | bytes 8388608 | tf_op jit(solution)/shard_map/all_to_all | solution.py:74
  330.2 20.3 %reshape.121 = bf16[2,16,16,4,32,32]{5,4,2,3,1,0:T(8,128)(2,1)} reshape(bf16[2,16,16,4,1024]{4,2,3,1,0:T(8,128)(2,1)} %copy.30) | data formatting | bytes 8388608 | tf_op jit(solution)/shard_map/reshape | solution.py:75
  350.5 30.9 %copy.38 = bf16[4,2,16,32,16,32]{3,2,0,5,4,1:T(8,128)(2,1)} copy(bf16[4,2,16,32,16,32]{5,3,2,0,4,1:T(8,128)(2,1)} %bitcast.65) | data formatting | bytes 8388608 | tf_op jit(solution)/shard_map/reshape | solution.py:77
  381.4 22.1 %reshape.198 = bf16[4,2,512,512]{2,0,3,1:T(4,128)(2,1)} reshape(bf16[4,2,16,32,16,32]{3,2,0,5,4,1:T(8,128)(2,1)} %copy.38) | data formatting | bytes 8388608 | tf_op jit(solution)/shard_map/reshape | solution.py:77
  403.5 25.4 %gather_fusion.1 = bf16[512,4,2,512]{3,1,2,0:T(4,128)(2,1)} fusion(bf16[4,2,512,512]{2,0,3,1:T(4,128)(2,1)} %reshape.198, s32[1024]{0:T(1024)S(1)} %pad_clamp_fusion), kind=kCustom, calls=%fused_computation.1 | custom fusion | bytes 8390656 | tf_op jit(solution)/shard_map/jit(_take)/gather | solution.py:81
  428.9 6.0 %select_bitcast_fusion = bf16[4,2,512,512]{2,0,1,3:T(4,128)(2,1)} fusion(bf16[512,4,2,512]{3,1,2,0:T(4,128)(2,1)} %gather_fusion.1, pred[512]{0:T(512)(128)(4,1)S(1)} %compare_and_fusion), kind=kLoop, calls=%fused_computation.41 | loop fusion | flops 2097152 | bytes 8389120 | tf_op jit(solution)/shard_map/jit(_take)/select_n | solution.py:81
  434.9 7.5 %copy.33 = bf16[4,2,512,512]{3,2,1,0:T(8,128)(2,1)} copy(bf16[4,2,512,512]{2,0,1,3:T(4,128)(2,1)} %select_bitcast_fusion) | data formatting | bytes 8388608
  442.4 47.3 %while.2 = (s32[]{:T(128)}, bf16[4,2,512,512]{3,2,1,0:T(8,128)(2,1)}, s32[10,3]{0,1:T(4,128)S(1)}, bf16[10,4,2,512,128]{3,4,0,1,2:T(8,128)(2,1)}, s32[]{:T(128)}) while((s32[]{:T(128)}, bf16[4,2,512,512]{3,2,1,0:T(8,128)(2,1)}, s32[10,3]{0,1:T(4,128)S(1)}, bf16[10,4,2,512,128]{3,4,0,1,2:T(8,128)(2,1)}, s32[]{:T(128)}) %tuple.54), condition=%wide.while_cond, body=%wide.while_body.sunk | while | flops 2 | bytes 6291569 | solution.py:88
  443.0 2.6 dynamic-slice_bitcast_fusion.5
  447.9 2.6 dynamic-slice_bitcast_fusion.5
  452.7 2.6 dynamic-slice_bitcast_fusion.5
  457.6 2.3 dynamic-slice_bitcast_fusion.5
  462.1 2.6 dynamic-slice_bitcast_fusion.5
  466.9 2.3 dynamic-slice_bitcast_fusion.5
  471.5 2.6 dynamic-slice_bitcast_fusion.5
  476.3 2.3 dynamic-slice_bitcast_fusion.5
  485.4 2.6 dynamic-slice_bitcast_fusion.5
  489.6 9.4 %slice_bitcast_fusion.3 = (bf16[4,10,512,128]{2,3,1,0:T(8,128)(2,1)}, bf16[4,10,512,128]{2,3,1,0:T(8,128)(2,1)}) fusion(bf16[4,10,2,512,128]{3,4,1,0,2:T(8,128)(2,1)} %bitcast.67), kind=kLoop, calls=%fused_computation.32 | loop fusion | bytes 20971520 | tf_op jit(solution)/shard_map/vmap(vmap())/squeeze | solution.py:90
  499.1 42.8 %while.3 = (s32[]{:T(128)}, bf16[4,2,512,512]{3,2,1,0:T(8,128)(2,1)}, s32[10,3]{0,1:T(4,128)S(1)}, bf16[10,4,2,512,128]{4,3,0,1,2:T(8,128)(2,1)}, s32[]{:T(128)}) while((s32[]{:T(128)}, bf16[4,2,512,512]{3,2,1,0:T(8,128)(2,1)}, s32[10,3]{0,1:T(4,128)S(1)}, bf16[10,4,2,512,128]{4,3,0,1,2:T(8,128)(2,1)}, s32[]{:T(128)}) %tuple.60), condition=%wide.while_cond.1, body=%wide.while_body.1.sunk | while | flops 2 | bytes 2097773 | solution.py:89
  499.7 3.7 copy_dynamic-update-slice_fusion.2
  504.0 3.6 copy_dynamic-update-slice_fusion.2
  508.3 3.6 copy_dynamic-update-slice_fusion.2
  512.6 3.7 copy_dynamic-update-slice_fusion.2
  516.9 3.7 copy_dynamic-update-slice_fusion.2
  521.2 3.7 copy_dynamic-update-slice_fusion.2
  525.6 3.7 copy_dynamic-update-slice_fusion.2
  529.9 3.7 copy_dynamic-update-slice_fusion.2
  534.3 3.3 copy_dynamic-update-slice_fusion.2
  538.2 3.7 copy_dynamic-update-slice_fusion.2
  541.9 9.3 %slice_bitcast_fusion.1 = (bf16[4,10,512,128]{3,2,1,0:T(8,128)(2,1)}, bf16[4,10,512,128]{3,2,1,0:T(8,128)(2,1)}) fusion(bf16[4,10,2,512,128]{4,3,1,0,2:T(8,128)(2,1)} %bitcast.66), kind=kLoop, calls=%fused_computation.30 | loop fusion | bytes 20971520 | tf_op jit(solution)/shard_map/vmap(vmap())/squeeze | solution.py:91
  551.2 12.2 %fusion = f32[4,10,256,256]{3,2,1,0:T(8,128)} fusion(bf16[4,10,512,128]{2,3,1,0:T(8,128)(2,1)} %get-tuple-element.66, bf16[4,10,512,128]{2,3,1,0:T(8,128)(2,1)} %get-tuple-element.65, bf16[4,10,512,128]{3,2,1,0:T(8,128)(2,1)} %get-tuple-element.64, bf16[4,10,512,128]{3,2,1,0:T(8,128)(2,1)} %get-tuple-element.63), kind=kOutput, calls=%fused_computation.9 | convolution fusion | flops 2726297600 | bytes 31457280 | tf_op jit(solution)/shard_map/vmap(vmap())/dot_general | solution.py:43
  563.4 5.2 fusion.33
  569.1 3.0 copy.37
  (87 shorter events, 38.0 us)
Async XLA Ops:
  0.0 38.3 %copy-start = (bf16[2,32,32768]{2,1,0:T(8,128)(2,1)S(1)}, bf16[2,32,32768]{2,1,0:T(8,128)(2,1)}, u32[]{:S(2)}) copy-start(bf16[2,32,32768]{2,1,0:T(8,128)(2,1)} %param.4) | copy-start | bytes 12582916
  1.8 36.5 %collective-permute-start = (bf16[2,32,15360]{2,1,0:T(8,128)(2,1)S(1)}, bf16[2,32,15360]{2,1,0:T(8,128)(2,1)S(1)}, u32[]{:S(2)}, u32[]{:S(2)}) collective-permute-start(bf16[2,32,15360]{2,1,0:T(8,128)(2,1)S(1)} %slice.136), channel_id=1, source_target_pairs={{0,16},{16,32},{32,48},{48,64},{64,80},{80,96},{96,112},{112,128},... | collective-permute-start | bytes 5898248 | tf_op jit(solution)/shard_map/ppermute | solution.py:14
  249.3 11.8 %copy-start.1 = (s32[10,2]{0,1:T(2,128)S(1)}, s32[10,2]{0,1:T(2,128)}, u32[]{:S(2)}) copy-start(s32[10,2]{0,1:T(2,128)} %param.7) | copy-start | bytes 244
  249.3 11.8 %copy-start.2 = (s32[256]{0:T(256)S(1)}, s32[256]{0:T(256)}, u32[]{:S(2)}) copy-start(s32[256]{0:T(256)} %param.6) | copy-start | bytes 3076
  249.3 73.2 %all-to-all-start.1 = ((bf16[2,16,16,4,1024]{4,3,1,0,2:T(4,128)(2,1)}), bf16[2,16,16,4,1024]{4,3,1,0,2:T(4,128)(2,1)}, u32[]{:S(2)}, u32[]{:S(2)}) async-start(bf16[2,16,16,4,1024]{4,3,1,0,2:T(4,128)(2,1)} %copy.29), calls=%async_computation.1 | async-start | bytes 8388608 | tf_op jit(solution)/shard_map/all_to_all | solution.py:74
where the time goes:
time: 584 us; the launch traced here: 573 us
  local copies, waits for them, and re-layouts  274 us (47%)
  blocking collectives  103 us (18%)
  other arithmetic  91.9 us (16%)
  waiting for transfers between devices  56.3 us (10%)
  matrix products  33.4 us (6%)
  starting transfers between devices  13.2 us (2%)
    all_to_all x1, blocking collectives, local(): lax.all_to_all(split_view, 'chan', split_axis=1, concat_axis=1, tiled=True)  103 us
    gather x80, local copies, waits for them, and re-layouts  89.9 us
    all_to_all x1, waiting for transfers between devices, local(): lax.all_to_all(by_owner, 'tm', split_axis=2, concat_axis=2, tiled=True)  56.3 us
    reshape x2, local copies, waits for them, and re-layouts, local(): jnp.transpose(received, (3, 0, 2, 4, 1, 5))  53 us
    transpose x1, other arithmetic, local(): filtered = jnp.swapaxes(summed.astype(jnp.bfloat16), 1, 2)  43.4 us
    another operation x2, other arithmetic  33.8 us
    gather x1, local copies, waits for them, and re-layouts, local(): per_channel = jnp.take(turned, input_slot, axis=3)  25.4 us
    dot_general x1, matrix products, local(): lax.dot_general(dft_table(channels), joined, (((0,), (1,)), ((), ())), pr...  21.2 us
  transfers between devices with their start and end apart: 2, of which 1 were waited for; matrix products, arithmetic and copies ran while one was open for 7% of the time, Pallas kernels for 0%

commit v1 on v0

v1 whole, which is shorter than its diff:
```python
import functools
import math

import jax
import jax.numpy as jnp
import numpy as np
from jax import lax
from jax.experimental import pallas as pl
from jax.experimental.pallas import tpu as pltpu
from jax.sharding import PartitionSpec as P

TILE = 128
OWNERS = ("chan", "tm")
NT = (((1,), (1,)), ((), ()))


def dft_rows(channels, per_owner):
    index = np.arange(channels, dtype=np.int32)
    angles = (index[:, None] * index[None, :] % channels).astype(np.float32)
    angles = angles * np.float32(2.0 * math.pi / channels)
    cosine = np.cos(angles) / np.float32(math.sqrt(channels))
    sine = np.sin(angles) / np.float32(math.sqrt(channels))
    real = np.concatenate([cosine, sine], 1)
    imag = np.concatenate([-sine, cosine], 1)
    return np.stack([real, imag], 1).reshape(2 * channels, 2 * channels).astype(jnp.bfloat16)


def front_kernel(
    first, frames, inputs, channels, sources, *refs
):
    n_in = 1 + max(s[0] for s in sources)
    hbm = refs[:n_in]
    taps_ref, table_hbm, out_ref = refs[n_in : n_in + 3]
    bufs = refs[n_in + 3 : 2 * n_in + 3]
    table_ref, joined, sems, table_sem = refs[2 * n_in + 3 :]
    tap_count = taps_ref.shape[0]
    half = 16
    groups = [(q, h) for q in range(2) for h in range(inputs // half)]
    spans = []
    for operand in range(n_in):
        used = [s[1] for s in sources if s[0] == operand]
        spans.append((min(used), max(used) + 1))

    def copies(at):
        q, h = groups[at]
        rows = pl.ds(h * half, half)
        return [
            pltpu.make_async_copy(
                hbm[p].at[q, rows, pl.ds(spans[p][0] * channels, (spans[p][1] - spans[p][0]) * channels)],
                bufs[p].at[q, rows],
                sems.at[p, at],
            )
            for p in range(n_in)
        ]

    for at in range(len(groups)):
        for copy in copies(at):
            copy.start()
    table_copy = pltpu.make_async_copy(table_hbm, table_ref, table_sem)
    table_copy.start()
    for at, (q, h) in enumerate(groups):
        for copy in copies(at):
            copy.wait()

        def columns(step, carry, q=q, h=h):
            lane = pl.multiple_of(step * 128, 128)
            taps = [taps_ref[pl.ds(t, 1), pl.ds(lane, 128)] for t in range(tap_count)]
            window = []
            for operand, frame in sources:
                place = pl.multiple_of((frame - spans[operand][0]) * channels + lane, 128)
                window.append(
                    bufs[operand][q, pl.ds(h * half, half), pl.ds(place, 128)].astype(jnp.float32)
                )
            for s in range(frames):
                total = window[s] * taps[0]
                for t in range(1, tap_count):
                    total = total + window[s + t] * taps[t]
                joined[pl.ds(s * inputs + h * half, half), pl.ds(pl.multiple_of(q * channels + lane, 128), 128)] = (
                    total.astype(jnp.bfloat16)
                )
            return carry

        lax.fori_loop(0, channels // 128, columns, 0)
    table_copy.wait()
    rows = 256

    def transform(step, carry):
        at = pl.ds(pl.multiple_of(step * rows, rows), rows)
        out_ref[at, :] = lax.dot_general(
            table_ref[at, :], joined[...], NT, preferred_element_type=jnp.float32
        ).astype(jnp.bfloat16)
        return carry

    lax.fori_loop(0, out_ref.shape[0] // rows, transform, 0)


def front(operands, taps, table, sources, frames):
    inputs = operands[0].shape[1]
    channels = taps.shape[1]
    n_in = len(operands)
    spans = []
    for operand in range(n_in):
        used = [s[1] for s in sources if s[0] == operand]
        spans.append(max(used) + 1 - min(used))
    size = 2 * channels
    return pl.pallas_call(
        functools.partial(front_kernel, 0, frames, inputs, channels, sources),
        out_shape=jax.ShapeDtypeStruct((size, frames * inputs), jnp.bfloat16),
        in_specs=[pl.BlockSpec(memory_space=pl.ANY)] * n_in
        + [pl.BlockSpec(memory_space=pltpu.VMEM), pl.BlockSpec(memory_space=pl.ANY)],
        out_specs=pl.BlockSpec(memory_space=pltpu.VMEM),
        scratch_shapes=[pltpu.VMEM((2, inputs, span * channels), jnp.bfloat16) for span in spans]
        + [
            pltpu.VMEM(table.shape, jnp.bfloat16),
            pltpu.VMEM((frames * inputs, size), jnp.bfloat16),
            pltpu.SemaphoreType.DMA((n_in, 2 * (inputs // 16))),
            pltpu.SemaphoreType.DMA,
        ],
        compiler_params=pltpu.CompilerParams(vmem_limit_bytes=40 * 2**20),
        cost_estimate=pl.CostEstimate(
            flops=2 * size * size * frames * inputs + 64 * frames * inputs * size,
            bytes_accessed=16 * 2**20,
            transcendentals=0,
        ),
        name="front",
    )(*operands, taps, table)


def sort_rows(times, parts):
    size = times * parts
    matrix = np.zeros((size, size), np.float32)
    for part in range(parts):
        for time in range(times):
            matrix[part * times + time, time * parts + part] = 1
    return matrix.astype(jnp.bfloat16)


def sort_lanes(group, block):
    size = group * group * block
    index = np.arange(size).reshape(group, group, block)
    matrix = np.zeros((size, size), np.float32)
    matrix[index.transpose(1, 0, 2).reshape(-1), np.arange(size)] = 1
    return matrix.astype(jnp.bfloat16)


def dot(left, right):
    return jnp.dot(left, right, preferred_element_type=jnp.float32).astype(jnp.bfloat16)


def gather_kernel(n_chan, n_time, parts, inputs, frames, got, rows_ref, lanes_ref, place_ref, out, sorted_rows, ordered):
    block = n_time * parts
    group = 128 // inputs
    for c in range(n_chan):
        at = pl.ds(c * block, block)
        sorted_rows[at, :] = dot(rows_ref[...], got[at, :])
    for a in range(n_chan // group):
        for g in range(frames // group):
            side = jnp.concatenate(
                [
                    sorted_rows[pl.ds((a * group + b) * block, block), pl.ds(g * 128, 128)]
                    for b in range(group)
                ],
                1,
            )
            turned = dot(side, lanes_ref[...])
            for j in range(group):
                for part in range(parts):
                    ordered[part, pl.ds((g * group + j) * n_time, n_time), pl.ds(a * 128, 128)] = turned[
                        part * n_time : (part + 1) * n_time, j * 128 : (j + 1) * 128
                    ]
    for part in range(parts):
        out[part] = lax.dot_general(
            place_ref[...], ordered[part], NT, preferred_element_type=jnp.float32
        ).astype(jnp.bfloat16)


def gather(got, rows, lanes, place, n_chan, n_time, parts, inputs):
    frames = got.shape[1] // inputs
    total = n_chan * inputs
    return pl.pallas_call(
        functools.partial(gather_kernel, n_chan, n_time, parts, inputs, frames),
        out_shape=jax.ShapeDtypeStruct((parts, total, n_time * frames), jnp.bfloat16),
        in_specs=[pl.BlockSpec(memory_space=pltpu.VMEM)] * 4,
        out_specs=pl.BlockSpec(memory_space=pltpu.VMEM),
        scratch_shapes=[
            pltpu.VMEM(got.shape, jnp.bfloat16),
            pltpu.VMEM((parts, n_time * frames, total), jnp.bfloat16),
        ],
        compiler_params=pltpu.CompilerParams(vmem_limit_bytes=32 * 2**20),
        cost_estimate=pl.CostEstimate(flops=4 * 10**9, bytes_accessed=8 * 2**20, transcendentals=0),
        name="gather",
    )(got, rows, lanes, place)


def correlate_kernel(scale, pairs, *refs):
    pieces, out = refs[:-1], refs[-1]
    for b in range(out.shape[1]):
        sides = []
        for end in range(2):
            at = pl.ds(pl.multiple_of(pairs[b, end] * TILE, TILE), TILE)
            sides.append([jnp.concatenate([piece[0, at, :], piece[1, at, :]], 0) for piece in pieces])
        gram = sum(
            lax.dot_general(left, right, NT, preferred_element_type=jnp.float32)
            for left, right in zip(*sides)
        )
        out[0, b, 0] = (gram[:TILE, :TILE] + gram[TILE:, TILE:]) * scale
        out[0, b, 1] = (gram[TILE:, :TILE] - gram[:TILE, TILE:]) * scale


def correlate(pieces, pair_blocks, scale):
    parts, inputs, times = pieces[0].shape
    blocks = pair_blocks.shape[0]
    return pl.pallas_call(
        functools.partial(correlate_kernel, scale),
        out_shape=jax.ShapeDtypeStruct((parts // 2, blocks, 2, TILE, TILE), jnp.float32),
        grid_spec=pltpu.PrefetchScalarGridSpec(
            num_scalar_prefetch=1,
            grid=(parts // 2,),
            in_specs=[pl.BlockSpec((2, inputs, times), lambda k, pairs: (k, 0, 0))] * len(pieces),
            out_specs=pl.BlockSpec((1, blocks, 2, TILE, TILE), lambda k, pairs: (k, 0, 0, 0, 0)),
        ),
        compiler_params=pltpu.CompilerParams(vmem_limit_bytes=32 * 2**20),
        name="correlate",
    )(pair_blocks, *pieces)


def local(voltages, filter_taps, slot_station, pair_blocks):
    tap_count, channels = filter_taps.shape
    inputs = voltages.shape[1]
    frame_count = voltages.shape[2] // channels
    n_chan = lax.axis_size("chan")
    n_time = lax.axis_size("tm")
    owners = n_chan * n_time
    per_owner = channels // owners
    parts = 2 * per_owner
    history = tap_count - 1
    tail = voltages[:, :, voltages.shape[2] - history * channels :]
    earlier = lax.ppermute(tail, "tm", [(i, i + 1) for i in range(n_time - 1)])
    table = jnp.asarray(dft_rows(channels, per_owner))
    cut = frame_count // 2

    def turn(spectra):
        pieces = spectra.reshape(owners, parts, -1)
        return lax.all_to_all(pieces, OWNERS, split_axis=0, concat_axis=0, tiled=True).reshape(owners * parts, -1)

    late = [(0, f) for f in range(cut - history, frame_count)]
    early = [(0, f) for f in range(history)] + [(1, f) for f in range(cut)]
    got_late = turn(front([voltages], filter_taps, table, late, frame_count - cut))
    got_early = turn(front([earlier, voltages], filter_taps, table, early, cut))

    total = n_chan * inputs
    index = jnp.arange(total, dtype=jnp.int32)
    station_in = jnp.repeat(slot_station, 2)
    place = (station_in[None, :] == index[:, None] // 2) & (index[None, :] % 2 == index[:, None] % 2)
    place = place.astype(jnp.bfloat16)
    rows = jnp.asarray(sort_rows(n_time, parts))
    lanes = jnp.asarray(sort_lanes(128 // inputs, inputs))
    pieces = [gather(got, rows, lanes, place, n_chan, n_time, parts, inputs) for got in (got_late, got_early)]
    return correlate(pieces, pair_blocks, 1.0 / (n_time * frame_count))


def solution(mesh):
    in_specs = (P(None, "chan", "tm"), P(), P(), P())
    out_specs = P(("chan", "tm"), None, None, None, None)
    return jax.shard_map(local, mesh=mesh, in_specs=in_specs, out_specs=out_specs, check_vma=False)
```

time: 584 us -> 174 us (0.30)
  the two profiles are of different devices: /device:TPU:29 before, /device:TPU:1 now
where the time goes in v1:
time: 174 us
  waiting for transfers between devices  86.6 us (50%)
  Pallas kernels  38.8 us (22%)
  starting transfers between devices  38.3 us (22%)
  local copies, waits for them, and re-layouts  9.91 us (6%)
    all_to_all x2, waiting for transfers between devices, turn(): lax.all_to_all(pieces, OWNERS, split_axis=0, concat_axis=0, tiled=True)  48.7 us
    ppermute x1, waiting for transfers between devices, local(): earlier = lax.ppermute(tail, 'tm', [(i, i + 1) for i in range(n_time - 1)])  37.9 us
    all_to_all x2, starting transfers between devices, turn(): lax.all_to_all(pieces, OWNERS, split_axis=0, concat_axis=0, tiled=True)  34.7 us
    pallas_call x2, Pallas kernels, front(): pl.pallas_call(functools.partial(front_kernel, 0, frames, inputs, channel...  25.7 us
    unnamed x23, local copies, waits for them, and re-layouts  7.97 us
    pallas_call x2, Pallas kernels, gather(): pl.pallas_call(functools.partial(gather_kernel, n_chan, n_time, parts, in...  7.6 us
    pallas_call x1, Pallas kernels, correlate(): pl.pallas_call(functools.partial(correlate_kernel, scale), out_shape=jax....  5.47 us
    ppermute x1, starting transfers between devices, local(): earlier = lax.ppermute(tail, 'tm', [(i, i + 1) for i in range(n_time - 1)])  3.54 us
  transfers between devices with their start and end apart: 3, of which 2 were waited for; matrix products, arithmetic and copies ran while one was open for 1% of the time, Pallas kernels for 10%

profile of v1, /device:TPU:1, one launch (start us, length us, event | category | flops | bytes accessed | tf_op | source)
XLA Modules:
  0.0 174.0 jit_solution(12507941821338287409)
XLA Ops:
  0.0 0.0 copy-start
  0.0 2.2 %copy-done = bf16[2,32,32768]{2,1,0:T(8,128)(2,1)S(1)} copy-done((bf16[2,32,32768]{2,1,0:T(8,128)(2,1)S(1)}, bf16[2,32,32768]{2,1,0:T(8,128)(2,1)}, u32[]{:S(2)}) %copy-start) | copy-done | bytes 4194328
  2.2 0.0 copy-start.5
  2.2 0.8 copy-done.5
  3.0 11.9 %front.2 = bf16[2048,512]{1,0:T(8,128)(2,1)S(1)} custom-call(bf16[2,32,32768]{2,1,0:T(8,128)(2,1)S(1)} %copy-done, f32[16,1024]{1,0:T(8,128)S(1)} %copy-done.5, bf16[2048,2048]{1,0:T(8,128)(2,1)} %constant.44.clone.refs_2_.refs_3_), custom_call_target="tpu_custom_call" | custom-call | flops 4362076160 | bytes 16777216 | tf_op jit(solution)/shard_map/front/pallas_call | solution.py:106
  14.9 0.0 copy-start.2
  14.9 1.3 copy-done.2
  16.2 15.7 %all-to-all-start = ((bf16[256,8,512]{2,1,0:T(8,128)(2,1)}), bf16[256,8,512]{2,1,0:T(8,128)(2,1)S(1)}, u32[]{:S(2)}, u32[]{:S(2)}) async-start(bf16[256,8,512]{2,1,0:T(8,128)(2,1)} %bitcast.5), calls=%async_computation | async-start | bytes 4194304 | tf_op jit(solution)/shard_map/all_to_all | solution.py:244
  31.9 0.0 copy-start.6
  31.9 1.7 slice.3
  33.6 3.5 %collective-permute-start = (bf16[2,32,15360]{2,1,0:T(8,128)(2,1)S(1)}, bf16[2,32,15360]{2,1,0:T(8,128)(2,1)S(1)}, u32[]{:S(2)}, u32[]{:S(2)}) collective-permute-start(bf16[2,32,15360]{2,1,0:T(8,128)(2,1)S(1)} %slice.3), channel_id=1, source_target_pairs={{0,16},{16,32},{32,48},{48,64},{64,80},{80,96},{96,112},{112,128},... | collective-permute-start | bytes 5898248 | tf_op jit(solution)/shard_map/ppermute | solution.py:238
  37.2 37.9 %collective-permute-done.refs_0_ = bf16[2,32,15360]{2,1,0:T(8,128)(2,1)S(1)} collective-permute-done((bf16[2,32,15360]{2,1,0:T(8,128)(2,1)S(1)}, bf16[2,32,15360]{2,1,0:T(8,128)(2,1)S(1)}, u32[]{:S(2)}, u32[]{:S(2)}) %collective-permute-start) | collective-permute-done | bytes 1966112 | tf_op jit(solution)/shard_map/ppermute | solution.py:238
  75.0 0.0 copy-done.6
  75.0 0.0 copy-start.1
  75.0 2.2 %copy-done.1 = bf16[2,32,32768]{2,1,0:T(8,128)(2,1)S(1)} copy-done((bf16[2,32,32768]{2,1,0:T(8,128)(2,1)S(1)}, bf16[2,32,32768]{2,1,0:T(8,128)(2,1)}, u32[]{:S(2)}) %copy-start.1) | copy-done | bytes 4194328
  77.2 13.8 %front.3 = bf16[2048,512]{1,0:T(8,128)(2,1)} custom-call(bf16[2,32,15360]{2,1,0:T(8,128)(2,1)S(1)} %collective-permute-done.refs_0_, bf16[2,32,32768]{2,1,0:T(8,128)(2,1)S(1)} %copy-done.1, f32[16,1024]{1,0:T(8,128)S(1)} %copy-done.6, bf16[2048,2048]{1,0:T(8,128)(2,1)} %constant.44.clone.refs_2_.refs_3_), custom_call_target="tpu_custom_call" | custom-call | flops 4362076160 | bytes 16777216 | tf_op jit(solution)/shard_map/front/pallas_call | solution.py:106
  91.1 0.0 all-to-all-done
  91.1 0.0 copy-start.10
  91.1 0.0 copy-start.9
  91.1 0.0 copy-start.7
  91.1 0.0 copy-start.8
  91.1 19.1 %all-to-all-start.1 = ((bf16[256,8,512]{2,1,0:T(8,128)(2,1)}), bf16[256,8,512]{2,1,0:T(8,128)(2,1)}, u32[]{:S(2)}, u32[]{:S(2)}) async-start(bf16[256,8,512]{2,1,0:T(8,128)(2,1)} %bitcast.2), calls=%async_computation.1 | async-start | bytes 4194304 | tf_op jit(solution)/shard_map/all_to_all | solution.py:244
  110.2 0.0 copy-done.10
  110.2 0.1 copy.9.pairs
  110.3 0.0 copy-done.9
  110.3 0.1 broadcast_in_dim.2
  110.4 0.1 eq.32
  110.6 0.2 and_convert_fusion.place_ref
  110.8 0.0 copy-done.7
  110.8 0.0 copy-done.8
  110.8 2.9 %gather.2.refs_0_ = bf16[8,512,256]{2,1,0:T(8,128)(2,1)S(1)} custom-call(bf16[2048,512]{1,0:T(8,128)(2,1)S(1)} %bitcast.4, bf16[128,128]{1,0:T(8,128)(2,1)S(1)} %copy-done.8, bf16[512,512]{1,0:T(8,128)(2,1)S(1)} %copy-done.7, bf16[512,512]{1,0:T(8,128)(2,1)S(1)} %and_convert_fusion.place_ref), custom_call_target="tpu_custom_call" | custom-call | flops 4000000000 | bytes 8388608 | tf_op jit(solution)/shard_map/gather/pallas_call | solution.py:180
  113.8 0.0 copy-start.3
  113.8 1.3 copy-done.3
  115.1 48.7 %all-to-all-done.1 = bf16[256,8,512]{2,1,0:T(8,128)(2,1)} async-done(((bf16[256,8,512]{2,1,0:T(8,128)(2,1)}), bf16[256,8,512]{2,1,0:T(8,128)(2,1)}, u32[]{:S(2)}, u32[]{:S(2)}) %all-to-all-start.1) | async-done | bytes 2097184 | tf_op jit(solution)/shard_map/all_to_all | solution.py:244
  163.8 0.0 copy-start.4
  163.8 4.7 %gather.3.refs_1_ = bf16[8,512,256]{2,1,0:T(8,128)(2,1)S(1)} custom-call(bf16[2048,512]{1,0:T(8,128)(2,1)} %bitcast.3.got, bf16[128,128]{1,0:T(8,128)(2,1)S(1)} %copy-done.8, bf16[512,512]{1,0:T(8,128)(2,1)S(1)} %copy-done.7, bf16[512,512]{1,0:T(8,128)(2,1)S(1)} %and_convert_fusion.place_ref), custom_call_target="tpu_custom_call" | custom-call | flops 4000000000 | bytes 8388608 | tf_op jit(solution)/shard_map/gather/pallas_call | solution.py:180
  168.5 0.0 copy-done.4
  168.5 5.5 %correlate.1 = f32[4,10,2,128,128]{4,3,2,1,0:T(8,128)} custom-call(s32[10,2]{1,0:T(8,128)S(1)} %copy.9.pairs, bf16[8,512,256]{2,1,0:T(8,128)(2,1)S(1)} %copy-done.4, bf16[8,512,256]{2,1,0:T(8,128)(2,1)S(1)} %gather.3.refs_1_), custom_call_target="tpu_custom_call" | custom-call | tf_op jit(solution)/shard_map/correlate/pallas_call | solution.py:213
  (1 shorter events, 0.0 us)
Async XLA Ops:
  0.0 2.2 %copy-start = (bf16[2,32,32768]{2,1,0:T(8,128)(2,1)S(1)}, bf16[2,32,32768]{2,1,0:T(8,128)(2,1)}, u32[]{:S(2)}) copy-start(bf16[2,32,32768]{2,1,0:T(8,128)(2,1)} %refs_1_.3) | copy-start | bytes 12582916
  2.2 0.8 copy-start.5
  14.9 1.3 copy-start.2
  16.2 74.8 %all-to-all-start = ((bf16[256,8,512]{2,1,0:T(8,128)(2,1)}), bf16[256,8,512]{2,1,0:T(8,128)(2,1)S(1)}, u32[]{:S(2)}, u32[]{:S(2)}) async-start(bf16[256,8,512]{2,1,0:T(8,128)(2,1)} %bitcast.5), calls=%async_computation | async-start | bytes 4194304 | tf_op jit(solution)/shard_map/all_to_all | solution.py:244
  31.9 43.1 %copy-start.6 = (f32[16,1024]{1,0:T(8,128)S(1)}, f32[16,1024]{1,0:T(8,128)}, u32[]{:S(2)}) copy-start(f32[16,1024]{1,0:T(8,128)} %refs_2_.2) | copy-start | bytes 196612
  33.6 41.4 %collective-permute-start = (bf16[2,32,15360]{2,1,0:T(8,128)(2,1)S(1)}, bf16[2,32,15360]{2,1,0:T(8,128)(2,1)S(1)}, u32[]{:S(2)}, u32[]{:S(2)}) collective-permute-start(bf16[2,32,15360]{2,1,0:T(8,128)(2,1)S(1)} %slice.3), channel_id=1, source_target_pairs={{0,16},{16,32},{32,48},{48,64},{64,80},{80,96},{96,112},{112,128},... | collective-permute-start | bytes 5898248 | tf_op jit(solution)/shard_map/ppermute | solution.py:238
  75.0 2.2 %copy-start.1 = (bf16[2,32,32768]{2,1,0:T(8,128)(2,1)S(1)}, bf16[2,32,32768]{2,1,0:T(8,128)(2,1)}, u32[]{:S(2)}) copy-start(bf16[2,32,32768]{2,1,0:T(8,128)(2,1)} %refs_1_.3) | copy-start | bytes 12582916
  91.1 19.1 %copy-start.10 = (s32[10,2]{0,1:T(2,128)S(1)}, s32[10,2]{0,1:T(2,128)}, u32[]{:S(2)}) copy-start(s32[10,2]{0,1:T(2,128)} %param.10) | copy-start | bytes 244
  91.1 19.2 %copy-start.9 = (s32[256]{0:T(256)S(1)}, s32[256]{0:T(256)}, u32[]{:S(2)}) copy-start(s32[256]{0:T(256)} %param.9) | copy-start | bytes 3076
  91.1 19.7 %copy-start.7 = (bf16[512,512]{1,0:T(8,128)(2,1)S(1)}, bf16[512,512]{1,0:T(8,128)(2,1)}, u32[]{:S(2)}) copy-start(bf16[512,512]{1,0:T(8,128)(2,1)} %constant.46.clone.lanes_ref) | copy-start | bytes 1572868
  91.1 19.7 %copy-start.8 = (bf16[128,128]{1,0:T(8,128)(2,1)S(1)}, bf16[128,128]{1,0:T(8,128)(2,1)}, u32[]{:S(2)}) copy-start(bf16[128,128]{1,0:T(8,128)(2,1)} %constant.45.clone.rows_ref) | copy-start | bytes 98308
  91.1 72.7 %all-to-all-start.1 = ((bf16[256,8,512]{2,1,0:T(8,128)(2,1)}), bf16[256,8,512]{2,1,0:T(8,128)(2,1)}, u32[]{:S(2)}, u32[]{:S(2)}) async-start(bf16[256,8,512]{2,1,0:T(8,128)(2,1)} %bitcast.2), calls=%async_computation.1 | async-start | bytes 4194304 | tf_op jit(solution)/shard_map/all_to_all | solution.py:244
  113.8 1.3 copy-start.3
  163.8 4.7 %copy-start.4 = (bf16[8,512,256]{2,1,0:T(8,128)(2,1)S(1)}, bf16[8,512,256]{2,1,0:T(8,128)(2,1)}, u32[]{:S(2)}) copy-start(bf16[8,512,256]{2,1,0:T(8,128)(2,1)} %copy-done.3) | copy-start | bytes 6291460

commit v2 on v1

--- a/solution.py
+++ b/solution.py
@@ -25,105 +25,132 @@
     return np.stack([real, imag], 1).reshape(2 * channels, 2 * channels).astype(jnp.bfloat16)
 
 
-def front_kernel(
-    first, frames, inputs, channels, sources, *refs
-):
-    n_in = 1 + max(s[0] for s in sources)
-    hbm = refs[:n_in]
-    taps_ref, table_hbm, out_ref = refs[n_in : n_in + 3]
-    bufs = refs[n_in + 3 : 2 * n_in + 3]
-    table_ref, joined, sems, table_sem = refs[2 * n_in + 3 :]
+STRIP = 8
+
+
+def strips(segments, n_in):
+    cuts, bounds = [], []
+    for operand in range(n_in):
+        used = [at for window in segments for where, at in window if where == operand]
+        first, last = min(used), max(used) + 1
+        bounds.append((first, last - first))
+        for start in range(first, last, STRIP):
+            cuts.append((operand, start, min(STRIP, last - start)))
+    return cuts, bounds
+
+
+def front_kernel(inputs, channels, segments, masked, n_in, *refs):
+    keep_ref, hbm = refs[0], refs[1 : 1 + n_in]
+    taps_ref, table_hbm, out_hbm = refs[1 + n_in : 4 + n_in]
+    bufs = refs[4 + n_in : 4 + 2 * n_in]
+    table_ref, joined, out, sems, table_sems, out_sems = refs[4 + 2 * n_in :]
     tap_count = taps_ref.shape[0]
     half = 16
     groups = [(q, h) for q in range(2) for h in range(inputs // half)]
-    spans = []
-    for operand in range(n_in):
-        used = [s[1] for s in sources if s[0] == operand]
-        spans.append((min(used), max(used) + 1))
+    cuts, bounds = strips(segments, n_in)
 
     def copies(at):
         q, h = groups[at]
         rows = pl.ds(h * half, half)
         return [
             pltpu.make_async_copy(
-                hbm[p].at[q, rows, pl.ds(spans[p][0] * channels, (spans[p][1] - spans[p][0]) * channels)],
-                bufs[p].at[q, rows],
-                sems.at[p, at],
+                hbm[p].at[q, rows, pl.ds(first * channels, count * channels)],
+                bufs[p].at[q, rows, pl.ds((first - bounds[p][0]) * channels, count * channels)],
+                sems.at[at, i],
             )
-            for p in range(n_in)
+            for i, (p, first, count) in enumerate(cuts)
         ]
+
+    size = table_ref.shape[0]
+    tile = size // table_sems.shape[0]
+
+    def table_copy(i):
+        at = pl.ds(i * tile, tile)
+        return pltpu.make_async_copy(table_hbm.at[at], table_ref.at[at], table_sems.at[i])
+
+    def filtered(q, h, step):
+        lane = pl.multiple_of(step * 128, 128)
+        rows = pl.ds(h * half, half)
+        taps = [taps_ref[pl.ds(t, 1), pl.ds(lane, 128)] for t in range(tap_count)]
+        base = 0
+        for number, window in enumerate(segments):
+            count = len(window) - tap_count + 1
+            totals = [None] * count
+            for at, (operand, frame) in enumerate(window):
+                place = pl.multiple_of((frame - bounds[operand][0]) * channels + lane, 128)
+                value = bufs[operand][q, rows, pl.ds(place, 128)].astype(jnp.float32)
+                if number == masked and at < tap_count - 1:
+                    value = value * keep_ref[0]
+                for s in range(max(0, at - tap_count + 1), min(count, at + 1)):
+                    term = value * taps[at - s]
+                    totals[s] = term if totals[s] is None else totals[s] + term
+                s = at - tap_count + 1
+                if s >= 0:
+                    joined[
+                        pl.ds((base + s) * inputs + h * half, half),
+                        pl.ds(pl.multiple_of(q * channels + lane, 128), 128),
+                    ] = totals[s].astype(jnp.bfloat16)
+            base += count
 
     for at in range(len(groups)):
         for copy in copies(at):
             copy.start()
-    table_copy = pltpu.make_async_copy(table_hbm, table_ref, table_sem)
-    table_copy.start()
     for at, (q, h) in enumerate(groups):
         for copy in copies(at):
             copy.wait()
+        if at == 0:
+            for i in range(table_sems.shape[0]):
+                table_copy(i).start()
 
         def columns(step, carry, q=q, h=h):
-            lane = pl.multiple_of(step * 128, 128)
-            taps = [taps_ref[pl.ds(t, 1), pl.ds(lane, 128)] for t in range(tap_count)]
-            window = []
-            for operand, frame in sources:
-                place = pl.multiple_of((frame - spans[operand][0]) * channels + lane, 128)
-                window.append(
-                    bufs[operand][q, pl.ds(h * half, half), pl.ds(place, 128)].astype(jnp.float32)
-                )
-            for s in range(frames):
-                total = window[s] * taps[0]
-                for t in range(1, tap_count):
-                    total = total + window[s + t] * taps[t]
-                joined[pl.ds(s * inputs + h * half, half), pl.ds(pl.multiple_of(q * channels + lane, 128), 128)] = (
-                    total.astype(jnp.bfloat16)
-                )
+            filtered(q, h, step)
             return carry
 
         lax.fori_loop(0, channels // 128, columns, 0)
-    table_copy.wait()
-    rows = 256
-
-    def transform(step, carry):
-        at = pl.ds(pl.multiple_of(step * rows, rows), rows)
-        out_ref[at, :] = lax.dot_general(
-            table_ref[at, :], joined[...], NT, preferred_element_type=jnp.float32
+    large = size // out_sems.shape[0]
+    sent = []
+    for i in range(out_sems.shape[0]):
+        rows = pl.ds(i * large, large)
+        for j in range(i * large // tile, (i + 1) * large // tile):
+            table_copy(j).wait()
+        out[rows, :] = lax.dot_general(
+            table_ref[rows, :], joined[...], NT, preferred_element_type=jnp.float32
         ).astype(jnp.bfloat16)
-        return carry
-
-    lax.fori_loop(0, out_ref.shape[0] // rows, transform, 0)
-
-
-def front(operands, taps, table, sources, frames):
+        sent.append(pltpu.make_async_copy(out.at[rows], out_hbm.at[rows], out_sems.at[i]))
+        sent[-1].start()
+    for copy in sent:
+        copy.wait()
+
+
+def front(keep, operands, taps, table, segments, masked):
     inputs = operands[0].shape[1]
     channels = taps.shape[1]
     n_in = len(operands)
-    spans = []
-    for operand in range(n_in):
-        used = [s[1] for s in sources if s[0] == operand]
-        spans.append(max(used) + 1 - min(used))
+    cuts, bounds = strips(segments, n_in)
     size = 2 * channels
+    lanes = inputs * sum(len(window) - taps.shape[0] + 1 for window in segments)
     return pl.pallas_call(
-        functools.partial(front_kernel, 0, frames, inputs, channels, sources),
-        out_shape=jax.ShapeDtypeStruct((size, frames * inputs), jnp.bfloat16),
-        in_specs=[pl.BlockSpec(memory_space=pl.ANY)] * n_in
+        functools.partial(front_kernel, inputs, channels, segments, masked, n_in),
+        out_shape=jax.ShapeDtypeStruct((size, lanes), jnp.bfloat16),
+        in_specs=[pl.BlockSpec(memory_space=pltpu.SMEM)]
+        + [pl.BlockSpec(memory_space=pl.ANY)] * n_in
         + [pl.BlockSpec(memory_space=pltpu.VMEM), pl.BlockSpec(memory_space=pl.ANY)],
-        out_specs=pl.BlockSpec(memory_space=pltpu.VMEM),
-        scratch_shapes=[pltpu.VMEM((2, inputs, span * channels), jnp.bfloat16) for span in spans]
+        out_specs=pl.BlockSpec(memory_space=pl.ANY),
+        scratch_shapes=[pltpu.VMEM((2, inputs, span * channels), jnp.bfloat16) for _, span in bounds]
         + [
             pltpu.VMEM(table.shape, jnp.bfloat16),
-            pltpu.VMEM((frames * inputs, size), jnp.bfloat16),
-            pltpu.SemaphoreType.DMA((n_in, 2 * (inputs // 16))),
-            pltpu.SemaphoreType.DMA,
+            pltpu.VMEM((lanes, size), jnp.bfloat16),
+            pltpu.VMEM((size, lanes), jnp.bfloat16),
+            pltpu.SemaphoreType.DMA((2 * (inputs // 16), len(cuts))),
+            pltpu.SemaphoreType.DMA((8,)),
+            pltpu.SemaphoreType.DMA((4,)),
         ],
-        compiler_params=pltpu.CompilerParams(vmem_limit_bytes=40 * 2**20),
+        compiler_params=pltpu.CompilerParams(vmem_limit_bytes=56 * 2**20),
         cost_estimate=pl.CostEstimate(
-            flops=2 * size * size * frames * inputs + 64 * frames * inputs * size,
-            bytes_accessed=16 * 2**20,
-            transcendentals=0,
+            flops=2 * size * size * lanes, bytes_accessed=16 * 2**20, transcendentals=0
         ),
         name="front",
-    )(*operands, taps, table)
+    )(keep, *operands, taps, table)
 
 
 def sort_rows(times, parts):
@@ -234,19 +261,30 @@
     per_owner = channels // owners
     parts = 2 * per_owner
     history = tap_count - 1
-    tail = voltages[:, :, voltages.shape[2] - history * channels :]
-    earlier = lax.ppermute(tail, "tm", [(i, i + 1) for i in range(n_time - 1)])
+    ahead = history // 2
+    cut = frame_count // 2
     table = jnp.asarray(dft_rows(channels, per_owner))
-    cut = frame_count // 2
+    t = lax.axis_index("tm")
+    keep = (t < n_time - 1).astype(jnp.float32).reshape(1)
 
     def turn(spectra):
         pieces = spectra.reshape(owners, parts, -1)
         return lax.all_to_all(pieces, OWNERS, split_axis=0, concat_axis=0, tiled=True).reshape(owners * parts, -1)
 
-    late = [(0, f) for f in range(cut - history, frame_count)]
-    early = [(0, f) for f in range(history)] + [(1, f) for f in range(cut)]
-    got_late = turn(front([voltages], filter_taps, table, late, frame_count - cut))
-    got_early = turn(front([earlier, voltages], filter_taps, table, early, cut))
+    late = [[(0, f) for f in range(cut - history, frame_count)]]
+    sent_late = front(keep, [voltages], filter_taps, table, late, None)
+    got_late = turn(sent_late)
+    behind = history - ahead
+    tail = voltages[:, :, (frame_count - behind) * channels :]
+    head = voltages[:, :, : ahead * channels]
+    before = lax.ppermute(tail, "tm", [(i, i + 1) for i in range(n_time - 1)])
+    after = lax.ppermute(head, "tm", [(i, (i - 1) % n_time) for i in range(n_time)])
+    operands, _ = lax.optimization_barrier(([before, voltages, after], sent_late))
+    early = [
+        [(0, f) for f in range(behind)] + [(1, f) for f in range(cut)],
+        [(1, f) for f in range(frame_count - history, frame_count)] + [(2, f) for f in range(ahead)],
+    ]
+    got_early = turn(front(keep, operands, filter_taps, table, early, 1))
 
     total = n_chan * inputs
     index = jnp.arange(total, dtype=jnp.int32)

time: 174 us -> 156 us (0.90)
  starting transfers between devices: 38.3 us -> 27.5 us
  waiting for transfers between devices: 86.6 us -> 81.3 us
  local copies, waits for them, and re-layouts: 9.91 us -> 6.11 us
    ppermute x1 -> x2, waiting for transfers between devices: 37.9 us -> 20.9 us  [the longest x1 20.9 us: local(): lax.ppermute(head, 'tm', [(i, (i - 1) % n_time) for i in range(n_time)])]
    all_to_all x2, waiting for transfers between devices: 48.7 us -> 60.4 us  [turn(): lax.all_to_all(pieces, OWNERS, split_axis=0, concat_axis=0, tiled=True)]
    all_to_all x2, starting transfers between devices: 34.7 us -> 23.9 us  [turn(): lax.all_to_all(pieces, OWNERS, split_axis=0, concat_axis=0, tiled=True)]
    unnamed x23 -> x17, local copies, waits for them, and re-layouts: 7.97 us -> 3.34 us
    ppermute x1 -> x2, starting transfers between devices: 3.54 us -> 3.63 us  [the longest x1 3.54 us: local(): before = lax.ppermute(tail, 'tm', [(i, i + 1) for i in range(n_time - 1)])]
  transfers between devices with their start and end apart: 3 -> 4, of which waited for: 2 -> 3; matrix products, arithmetic and copies ran while one was open for 1% -> 2% of each run, Pallas kernels for 10% -> 11%
where the time goes in v2:
time: 156 us
  waiting for transfers between devices  81.3 us (52%)
  Pallas kernels  40.3 us (26%)
  starting transfers between devices  27.5 us (18%)
  local copies, waits for them, and re-layouts  6.11 us (4%)
    all_to_all x2, waiting for transfers between devices, turn(): lax.all_to_all(pieces, OWNERS, split_axis=0, concat_axis=0, tiled=True)  60.4 us
    pallas_call x2, Pallas kernels, front(): pl.pallas_call(functools.partial(front_kernel, inputs, channels, segments...  27.2 us
    all_to_all x2, starting transfers between devices, turn(): lax.all_to_all(pieces, OWNERS, split_axis=0, concat_axis=0, tiled=True)  23.9 us
    ppermute x1, waiting for transfers between devices, local(): lax.ppermute(head, 'tm', [(i, (i - 1) % n_time) for i in range(n_time)])  20.9 us
    pallas_call x2, Pallas kernels, gather(): pl.pallas_call(functools.partial(gather_kernel, n_chan, n_time, parts, in...  7.59 us
    pallas_call x1, Pallas kernels, correlate(): pl.pallas_call(functools.partial(correlate_kernel, scale), out_shape=jax....  5.46 us
    ppermute x1, starting transfers between devices, local(): before = lax.ppermute(tail, 'tm', [(i, i + 1) for i in range(n_time - 1)])  3.54 us
    unnamed x17, local copies, waits for them, and re-layouts  3.34 us
  transfers between devices with their start and end apart: 4, of which 3 were waited for; matrix products, arithmetic and copies ran while one was open for 2% of the time, Pallas kernels for 11%

profile of v2, /device:TPU:1, one launch (start us, length us, event | category | flops | bytes accessed | tf_op | source)
XLA Modules:
  0.0 155.6 jit_solution(4115317438245321276)
XLA Ops:
  0.0 13.3 %front.2 = bf16[2048,512]{1,0:T(8,128)(2,1)} custom-call(f32[1]{0:T(128)} %bitcast.refs_0_, bf16[2,32,32768]{2,1,0:T(8,128)(2,1)} %refs_2_.2, f32[16,1024]{1,0:T(8,128)} %refs_4_.1, bf16[2048,2048]{1,0:T(8,128)(2,1)} %constant.51.clone.refs_3_.refs_5_), custom_call_target="tpu_custom_call" | custom-call | flops 4294967296 | bytes 16777216 | tf_op jit(solution)/shard_map/front/pallas_call | solution.py:132
  13.3 15.7 %all-to-all-start = ((bf16[256,8,512]{2,1,0:T(8,128)(2,1)}), bf16[256,8,512]{2,1,0:T(8,128)(2,1)S(1)}, u32[]{:S(2)}, u32[]{:S(2)}) async-start(bf16[256,8,512]{2,1,0:T(8,128)(2,1)} %bitcast.7), calls=%async_computation | async-start | bytes 4194304 | tf_op jit(solution)/shard_map/all_to_all | solution.py:272
  29.0 1.3 slice.6
  30.3 3.5 %collective-permute-start = (bf16[2,32,8192]{2,1,0:T(8,128)(2,1)S(1)}, bf16[2,32,8192]{2,1,0:T(8,128)(2,1)S(1)}, u32[]{:S(2)}, u32[]{:S(2)}) collective-permute-start(bf16[2,32,8192]{2,1,0:T(8,128)(2,1)S(1)} %slice.6), channel_id=1, source_target_pairs={{0,16},{16,32},{32,48},{48,64},{64,80},{80,96},{96,112},{112,128},... | collective-permute-start | bytes 3145736 | tf_op jit(solution)/shard_map/ppermute | solution.py:280
  33.8 1.2 slice.7
  35.1 0.1 collective-permute-start.1
  35.2 20.9 %collective-permute-done.1.refs_3_ = bf16[2,32,7168]{2,1,0:T(8,128)(2,1)S(1)} collective-permute-done((bf16[2,32,7168]{2,1,0:T(8,128)(2,1)S(1)}, bf16[2,32,7168]{2,1,0:T(8,128)(2,1)S(1)}, u32[]{:S(2)}, u32[]{:S(2)}) %collective-permute-start.1) | collective-permute-done | bytes 917536 | tf_op jit(solution)/shard_map/ppermute | solution.py:281
  56.1 0.0 copy-start.5
  56.1 0.0 collective-permute-done.refs_1_
  56.1 0.9 copy-done.5
  57.0 0.0 copy-start.4
  57.0 1.0 copy-done.4
  58.0 13.9 %front.3 = bf16[2048,512]{1,0:T(8,128)(2,1)} custom-call(f32[1]{0:T(128)} %bitcast.refs_0_, bf16[2,32,8192]{2,1,0:T(8,128)(2,1)} %copy-done.4, bf16[2,32,32768]{2,1,0:T(8,128)(2,1)} %refs_2_.2, bf16[2,32,7168]{2,1,0:T(8,128)(2,1)} %copy-done.5, f32[16,1024]{1,0:T(8,128)} %refs_4_.1, bf16[2048,2048]{1,0:T(8,128)(2,1)} %constant.51.clone.refs_3_.refs_5_), custom_call_target="tpu_custom_call" | custom-call | flops 4294967296 | bytes 16777216 | tf_op jit(solution)/shard_map/front/pallas_call | solution.py:132
  71.9 11.6 %all-to-all-done = bf16[256,8,512]{2,1,0:T(8,128)(2,1)S(1)} async-done(((bf16[256,8,512]{2,1,0:T(8,128)(2,1)}), bf16[256,8,512]{2,1,0:T(8,128)(2,1)S(1)}, u32[]{:S(2)}, u32[]{:S(2)}) %all-to-all-start) | async-done | bytes 2097184 | tf_op jit(solution)/shard_map/all_to_all | solution.py:272
  83.5 0.0 copy-start.7
  83.5 0.0 copy-start.6
  83.5 0.0 copy-start.2
  83.5 0.0 copy-start.3
  83.5 8.2 %all-to-all-start.1 = ((bf16[256,8,512]{2,1,0:T(8,128)(2,1)}), bf16[256,8,512]{2,1,0:T(8,128)(2,1)}, u32[]{:S(2)}, u32[]{:S(2)}) async-start(bf16[256,8,512]{2,1,0:T(8,128)(2,1)} %bitcast.6), calls=%async_computation.1 | async-start | bytes 4194304 | tf_op jit(solution)/shard_map/all_to_all | solution.py:272
  91.7 0.0 copy-done.7
  91.7 0.1 copy.9.pairs
  91.8 0.0 copy-done.6
  91.8 0.1 broadcast_in_dim.2
  91.9 0.1 eq.32
  92.1 0.2 and_convert_fusion.place_ref
  92.3 0.0 copy-done.2
  92.3 0.0 copy-done.3
  92.3 2.9 %gather.2.refs_0_ = bf16[8,512,256]{2,1,0:T(8,128)(2,1)S(1)} custom-call(bf16[2048,512]{1,0:T(8,128)(2,1)S(1)} %bitcast.5, bf16[128,128]{1,0:T(8,128)(2,1)S(1)} %copy-done.3, bf16[512,512]{1,0:T(8,128)(2,1)S(1)} %copy-done.2, bf16[512,512]{1,0:T(8,128)(2,1)S(1)} %and_convert_fusion.place_ref), custom_call_target="tpu_custom_call" | custom-call | flops 4000000000 | bytes 8388608 | tf_op jit(solution)/shard_map/gather/pallas_call | solution.py:207
  95.3 0.0 copy-start
  95.3 1.3 copy-done
  96.6 48.9 %all-to-all-done.1 = bf16[256,8,512]{2,1,0:T(8,128)(2,1)} async-done(((bf16[256,8,512]{2,1,0:T(8,128)(2,1)}), bf16[256,8,512]{2,1,0:T(8,128)(2,1)}, u32[]{:S(2)}, u32[]{:S(2)}) %all-to-all-start.1) | async-done | bytes 2097184 | tf_op jit(solution)/shard_map/all_to_all | solution.py:272
  145.4 0.0 copy-start.1
  145.4 4.7 %gather.3.refs_1_ = bf16[8,512,256]{2,1,0:T(8,128)(2,1)S(1)} custom-call(bf16[2048,512]{1,0:T(8,128)(2,1)} %bitcast.4.got, bf16[128,128]{1,0:T(8,128)(2,1)S(1)} %copy-done.3, bf16[512,512]{1,0:T(8,128)(2,1)S(1)} %copy-done.2, bf16[512,512]{1,0:T(8,128)(2,1)S(1)} %and_convert_fusion.place_ref), custom_call_target="tpu_custom_call" | custom-call | flops 4000000000 | bytes 8388608 | tf_op jit(solution)/shard_map/gather/pallas_call | solution.py:207
  150.1 0.0 copy-done.1
  150.1 5.5 %correlate.1 = f32[4,10,2,128,128]{4,3,2,1,0:T(8,128)} custom-call(s32[10,2]{1,0:T(8,128)S(1)} %copy.9.pairs, bf16[8,512,256]{2,1,0:T(8,128)(2,1)S(1)} %copy-done.1, bf16[8,512,256]{2,1,0:T(8,128)(2,1)S(1)} %gather.3.refs_1_), custom_call_target="tpu_custom_call" | custom-call | tf_op jit(solution)/shard_map/correlate/pallas_call | solution.py:240
  (1 shorter events, 0.0 us)
Async XLA Ops:
  13.3 70.2 %all-to-all-start = ((bf16[256,8,512]{2,1,0:T(8,128)(2,1)}), bf16[256,8,512]{2,1,0:T(8,128)(2,1)S(1)}, u32[]{:S(2)}, u32[]{:S(2)}) async-start(bf16[256,8,512]{2,1,0:T(8,128)(2,1)} %bitcast.7), calls=%async_computation | async-start | bytes 4194304 | tf_op jit(solution)/shard_map/all_to_all | solution.py:272
  30.3 25.8 %collective-permute-start = (bf16[2,32,8192]{2,1,0:T(8,128)(2,1)S(1)}, bf16[2,32,8192]{2,1,0:T(8,128)(2,1)S(1)}, u32[]{:S(2)}, u32[]{:S(2)}) collective-permute-start(bf16[2,32,8192]{2,1,0:T(8,128)(2,1)S(1)} %slice.6), channel_id=1, source_target_pairs={{0,16},{16,32},{32,48},{48,64},{64,80},{80,96},{96,112},{112,128},... | collective-permute-start | bytes 3145736 | tf_op jit(solution)/shard_map/ppermute | solution.py:280
  35.1 21.0 %collective-permute-start.1 = (bf16[2,32,7168]{2,1,0:T(8,128)(2,1)S(1)}, bf16[2,32,7168]{2,1,0:T(8,128)(2,1)S(1)}, u32[]{:S(2)}, u32[]{:S(2)}) collective-permute-start(bf16[2,32,7168]{2,1,0:T(8,128)(2,1)S(1)} %slice.7), channel_id=1, source_target_pairs={{0,240},{16,0},{32,16},{48,32},{64,48},{80,64},{96,80},{112,96},{1... | collective-permute-start | bytes 2752520 | tf_op jit(solution)/shard_map/ppermute | solution.py:281
  56.1 1.0 copy-start.5
  57.0 1.0 copy-start.4
  83.5 8.2 %copy-start.7 = (s32[10,2]{0,1:T(2,128)S(1)}, s32[10,2]{0,1:T(2,128)}, u32[]{:S(2)}) copy-start(s32[10,2]{0,1:T(2,128)} %param.10) | copy-start | bytes 244
  83.5 8.3 %copy-start.6 = (s32[256]{0:T(256)S(1)}, s32[256]{0:T(256)}, u32[]{:S(2)}) copy-start(s32[256]{0:T(256)} %param.9) | copy-start | bytes 3076
  83.5 8.8 %copy-start.2 = (bf16[512,512]{1,0:T(8,128)(2,1)S(1)}, bf16[512,512]{1,0:T(8,128)(2,1)}, u32[]{:S(2)}) copy-start(bf16[512,512]{1,0:T(8,128)(2,1)} %constant.53.clone.lanes_ref) | copy-start | bytes 1572868
  83.5 8.8 %copy-start.3 = (bf16[128,128]{1,0:T(8,128)(2,1)S(1)}, bf16[128,128]{1,0:T(8,128)(2,1)}, u32[]{:S(2)}) copy-start(bf16[128,128]{1,0:T(8,128)(2,1)} %constant.52.clone.rows_ref) | copy-start | bytes 98308
  83.5 62.0 %all-to-all-start.1 = ((bf16[256,8,512]{2,1,0:T(8,128)(2,1)}), bf16[256,8,512]{2,1,0:T(8,128)(2,1)}, u32[]{:S(2)}, u32[]{:S(2)}) async-start(bf16[256,8,512]{2,1,0:T(8,128)(2,1)} %bitcast.6), calls=%async_computation.1 | async-start | bytes 4194304 | tf_op jit(solution)/shard_map/all_to_all | solution.py:272
  95.3 1.3 copy-start
  145.4 4.7 %copy-start.1 = (bf16[8,512,256]{2,1,0:T(8,128)(2,1)S(1)}, bf16[8,512,256]{2,1,0:T(8,128)(2,1)}, u32[]{:S(2)}) copy-start(bf16[8,512,256]{2,1,0:T(8,128)(2,1)} %copy-done) | copy-start | bytes 6291460

commit v3 on v2

--- a/solution.py
+++ b/solution.py
@@ -14,15 +14,17 @@
 NT = (((1,), (1,)), ((), ()))
 
 
-def dft_rows(channels, per_owner):
+def dft_half(channels, per_owner):
     index = np.arange(channels, dtype=np.int32)
     angles = (index[:, None] * index[None, :] % channels).astype(np.float32)
     angles = angles * np.float32(2.0 * math.pi / channels)
-    cosine = np.cos(angles) / np.float32(math.sqrt(channels))
-    sine = np.sin(angles) / np.float32(math.sqrt(channels))
-    real = np.concatenate([cosine, sine], 1)
-    imag = np.concatenate([-sine, cosine], 1)
-    return np.stack([real, imag], 1).reshape(2 * channels, 2 * channels).astype(jnp.bfloat16)
+    half = channels // 2
+    tiles = np.arange(half).reshape(2, -1, per_owner).transpose(1, 0, 2).reshape(-1)
+    last = np.zeros(16, np.int32)
+    last[0], last[per_owner] = half // 2, half
+    picked = np.concatenate([tiles, last])
+    tables = [f(angles[picked]) / np.float32(math.sqrt(channels)) for f in (np.cos, np.sin)]
+    return np.concatenate(tables, 0).astype(jnp.bfloat16)
 
 
 STRIP = 8
@@ -61,11 +63,9 @@
             for i, (p, first, count) in enumerate(cuts)
         ]
 
-    size = table_ref.shape[0]
-    tile = size // table_sems.shape[0]
-
     def table_copy(i):
-        at = pl.ds(i * tile, tile)
+        size = table_ref.shape[0] // table_sems.shape[0]
+        at = pl.ds(i * size, size)
         return pltpu.make_async_copy(table_hbm.at[at], table_ref.at[at], table_sems.at[i])
 
     def filtered(q, h, step):
@@ -86,10 +86,9 @@
                     totals[s] = term if totals[s] is None else totals[s] + term
                 s = at - tap_count + 1
                 if s >= 0:
-                    joined[
-                        pl.ds((base + s) * inputs + h * half, half),
-                        pl.ds(pl.multiple_of(q * channels + lane, 128), 128),
-                    ] = totals[s].astype(jnp.bfloat16)
+                    joined[q, pl.ds((base + s) * inputs + h * half, half), pl.ds(lane, 128)] = totals[s].astype(
+                        jnp.bfloat16
+                    )
             base += count
 
     for at in range(len(groups)):
@@ -106,20 +105,49 @@
             filtered(q, h, step)
             return carry
 
-        lax.fori_loop(0, channels // 128, columns, 0)
-    large = size // out_sems.shape[0]
+        lax.fori_loop(0, channels // 128, columns, 0, unroll=2)
+    for i in range(table_sems.shape[0]):
+        table_copy(i).wait()
+    count = table_ref.shape[0] // 2
+    used = count - 16
+    low = lax.broadcasted_iota(jnp.int32, (used // 8, 8, SIDE), 1)
+    first, upper = low % 4 == 0, low < 4
+
+    def product(table, q, side):
+        return lax.dot_general(
+            table_ref[pl.ds(table * count, count), :],
+            joined[q, side, :],
+            NT,
+            preferred_element_type=jnp.float32,
+        ).reshape(count // 8, 8, SIDE)
+
+    def swapped(value):
+        return jnp.concatenate([value[:, 4:], value[:, :4]], 1)
+
     sent = []
-    for i in range(out_sems.shape[0]):
-        rows = pl.ds(i * large, large)
-        for j in range(i * large // tile, (i + 1) * large // tile):
-            table_copy(j).wait()
-        out[rows, :] = lax.dot_general(
-            table_ref[rows, :], joined[...], NT, preferred_element_type=jnp.float32
-        ).astype(jnp.bfloat16)
-        sent.append(pltpu.make_async_copy(out.at[rows], out_hbm.at[rows], out_sems.at[i]))
+    for i in range(joined.shape[1] // SIDE):
+        side = pl.ds(i * SIDE, SIDE)
+        cosines = [product(0, q, side) for q in range(2)]
+        sines = [product(1, q, side) for q in range(2)]
+        sums = [cosines[0] + sines[1], cosines[1] - sines[0]]
+        mirrored = [cosines[0] - sines[1], cosines[1] + sines[0]]
+        sums = [x[: used // 8] for x in sums]
+        mirrored = [jnp.where(first, x[1 : used // 8 + 1], x[: used // 8]) for x in mirrored]
+        at = 0
+        for real, imag in (sums, mirrored):
+            for piece in (
+                jnp.where(upper, real, swapped(imag)),
+                jnp.where(upper, swapped(real), imag),
+            ):
+                out[pl.ds(at, used), side] = piece.reshape(used, SIDE).astype(jnp.bfloat16)
+                at += used
+        sent.append(pltpu.make_async_copy(out.at[:, side], out_hbm.at[:, side], out_sems.at[i]))
         sent[-1].start()
     for copy in sent:
         copy.wait()
+
+
+SIDE = 256
 
 
 def front(keep, operands, taps, table, segments, masked):
@@ -139,15 +167,15 @@
         scratch_shapes=[pltpu.VMEM((2, inputs, span * channels), jnp.bfloat16) for _, span in bounds]
         + [
             pltpu.VMEM(table.shape, jnp.bfloat16),
-            pltpu.VMEM((lanes, size), jnp.bfloat16),
+            pltpu.VMEM((2, lanes, channels), jnp.bfloat16),
             pltpu.VMEM((size, lanes), jnp.bfloat16),
             pltpu.SemaphoreType.DMA((2 * (inputs // 16), len(cuts))),
-            pltpu.SemaphoreType.DMA((8,)),
-            pltpu.SemaphoreType.DMA((4,)),
+            pltpu.SemaphoreType.DMA((2,)),
+            pltpu.SemaphoreType.DMA((lanes // SIDE,)),
         ],
-        compiler_params=pltpu.CompilerParams(vmem_limit_bytes=56 * 2**20),
+        compiler_params=pltpu.CompilerParams(vmem_limit_bytes=62 * 2**20),
         cost_estimate=pl.CostEstimate(
-            flops=2 * size * size * lanes, bytes_accessed=16 * 2**20, transcendentals=0
+            flops=size * size * lanes, bytes_accessed=16 * 2**20, transcendentals=0
         ),
         name="front",
     )(keep, *operands, taps, table)
@@ -155,10 +183,11 @@
 
 def sort_rows(times, parts):
     size = times * parts
-    matrix = np.zeros((size, size), np.float32)
+    matrix = np.zeros((2, size, size), np.float32)
     for part in range(parts):
         for time in range(times):
-            matrix[part * times + time, time * parts + part] = 1
+            matrix[0, part * times + time, time * parts + part] = 1
+            matrix[1, part * times + time, (times - 1 - time) * parts + part] = 1
     return matrix.astype(jnp.bfloat16)
 
 
@@ -174,12 +203,19 @@
     return jnp.dot(left, right, preferred_element_type=jnp.float32).astype(jnp.bfloat16)
 
 
-def gather_kernel(n_chan, n_time, parts, inputs, frames, got, rows_ref, lanes_ref, place_ref, out, sorted_rows, ordered):
-    block = n_time * parts
-    group = 128 // inputs
+def dot_nt(left, right):
+    return lax.dot_general(left, right, NT, preferred_element_type=jnp.float32).astype(jnp.bfloat16)
+
+
+def gather_kernel(n_chan, got, rows_ref, lanes_ref, place_ref, out, sorted_rows, ordered):
+    parts, times, total = ordered.shape
+    block = got.shape[0] // n_chan
+    n_time = block // parts
+    frames = times // n_time
+    group = 128 // (total // n_chan)
     for c in range(n_chan):
         at = pl.ds(c * block, block)
-        sorted_rows[at, :] = dot(rows_ref[...], got[at, :])
+        sorted_rows[at, :] = dot(rows_ref[c // (n_chan // 2)], got[at, :])
     for a in range(n_chan // group):
         for g in range(frames // group):
             side = jnp.concatenate(
@@ -196,36 +232,39 @@
                         part * n_time : (part + 1) * n_time, j * 128 : (j + 1) * 128
                     ]
     for part in range(parts):
-        out[part] = lax.dot_general(
-            place_ref[...], ordered[part], NT, preferred_element_type=jnp.float32
-        ).astype(jnp.bfloat16)
-
-
-def gather(got, rows, lanes, place, n_chan, n_time, parts, inputs):
-    frames = got.shape[1] // inputs
-    total = n_chan * inputs
+        out[part // out.shape[1], part % out.shape[1]] = dot_nt(place_ref[...], ordered[part])
+
+
+def gather(got, rows, lanes, place, n_chan, n_time, parts, limit):
+    total = place.shape[0]
+    times = n_time * got.shape[1] // (total // n_chan)
     return pl.pallas_call(
-        functools.partial(gather_kernel, n_chan, n_time, parts, inputs, frames),
-        out_shape=jax.ShapeDtypeStruct((parts, total, n_time * frames), jnp.bfloat16),
+        functools.partial(gather_kernel, n_chan),
+        out_shape=jax.ShapeDtypeStruct((2, parts // 2, total, times), jnp.bfloat16),
         in_specs=[pl.BlockSpec(memory_space=pltpu.VMEM)] * 4,
         out_specs=pl.BlockSpec(memory_space=pltpu.VMEM),
         scratch_shapes=[
             pltpu.VMEM(got.shape, jnp.bfloat16),
-            pltpu.VMEM((parts, n_time * frames, total), jnp.bfloat16),
+            pltpu.VMEM((parts, times, total), jnp.bfloat16),
         ],
-        compiler_params=pltpu.CompilerParams(vmem_limit_bytes=32 * 2**20),
+        compiler_params=pltpu.CompilerParams(vmem_limit_bytes=limit),
         cost_estimate=pl.CostEstimate(flops=4 * 10**9, bytes_accessed=8 * 2**20, transcendentals=0),
         name="gather",
     )(got, rows, lanes, place)
 
 
-def correlate_kernel(scale, pairs, *refs):
+LIMIT = 20 * 2**20
+LIMIT_A = 56 * 2**20
+LIMIT_B = 20 * 2**20
+
+
+def correlate_kernel(scale, scalars, *refs):
     pieces, out = refs[:-1], refs[-1]
     for b in range(out.shape[1]):
         sides = []
         for end in range(2):
-            at = pl.ds(pl.multiple_of(pairs[b, end] * TILE, TILE), TILE)
-            sides.append([jnp.concatenate([piece[0, at, :], piece[1, at, :]], 0) for piece in pieces])
+            at = pl.ds(pl.multiple_of(scalars[2 * b + end] * TILE, TILE), TILE)
+            sides.append([jnp.concatenate([piece[0, 0, at, :], piece[1, 0, at, :]], 0) for piece in pieces])
         gram = sum(
             lax.dot_general(left, right, NT, preferred_element_type=jnp.float32)
             for left, right in zip(*sides)
@@ -234,21 +273,28 @@
         out[0, b, 1] = (gram[TILE:, :TILE] - gram[:TILE, TILE:]) * scale
 
 
-def correlate(pieces, pair_blocks, scale):
-    parts, inputs, times = pieces[0].shape
+def correlate(pieces, pair_blocks, upper, scale):
+    per_owner = pieces[0].shape[1]
     blocks = pair_blocks.shape[0]
+    scalars = jnp.concatenate([pair_blocks.reshape(-1), upper.astype(jnp.int32).reshape(1)])
+
+    def channel_of(j, scalars):
+        return jnp.where(scalars[2 * blocks] > 0, lax.rem(per_owner - j, per_owner), j)
+
     return pl.pallas_call(
         functools.partial(correlate_kernel, scale),
-        out_shape=jax.ShapeDtypeStruct((parts // 2, blocks, 2, TILE, TILE), jnp.float32),
+        out_shape=jax.ShapeDtypeStruct((per_owner, blocks, 2, TILE, TILE), jnp.float32),
         grid_spec=pltpu.PrefetchScalarGridSpec(
             num_scalar_prefetch=1,
-            grid=(parts // 2,),
-            in_specs=[pl.BlockSpec((2, inputs, times), lambda k, pairs: (k, 0, 0))] * len(pieces),
-            out_specs=pl.BlockSpec((1, blocks, 2, TILE, TILE), lambda k, pairs: (k, 0, 0, 0, 0)),
+            grid=(per_owner,),
+            in_specs=[pl.BlockSpec((2, 1) + x.shape[2:], lambda j, scalars: (0, j, 0, 0)) for x in pieces],
+            out_specs=pl.BlockSpec(
+                (1, blocks, 2, TILE, TILE), lambda j, scalars: (channel_of(j, scalars), 0, 0, 0, 0)
+            ),
         ),
-        compiler_params=pltpu.CompilerParams(vmem_limit_bytes=32 * 2**20),
+        compiler_params=pltpu.CompilerParams(vmem_limit_bytes=LIMIT),
         name="correlate",
-    )(pair_blocks, *pieces)
+    )(scalars, *pieces)
 
 
 def local(voltages, filter_taps, slot_station, pair_blocks):
@@ -263,13 +309,18 @@
     history = tap_count - 1
     ahead = history // 2
     cut = frame_count // 2
-    table = jnp.asarray(dft_rows(channels, per_owner))
+    table = jnp.asarray(dft_half(channels, per_owner))
     t = lax.axis_index("tm")
     keep = (t < n_time - 1).astype(jnp.float32).reshape(1)
 
+    ranks = list(range(owners // 2)) + list(range(owners - 1, owners // 2 - 1, -1))
+
     def turn(spectra):
         pieces = spectra.reshape(owners, parts, -1)
-        return lax.all_to_all(pieces, OWNERS, split_axis=0, concat_axis=0, tiled=True).reshape(owners * parts, -1)
+        got = lax.all_to_all(
+            pieces, OWNERS, split_axis=0, concat_axis=0, tiled=True, axis_index_groups=[ranks]
+        )
+        return got.reshape(owners * parts, -1)
 
     late = [[(0, f) for f in range(cut - history, frame_count)]]
     sent_late = front(keep, [voltages], filter_taps, table, late, None)
@@ -288,13 +339,19 @@
 
     total = n_chan * inputs
     index = jnp.arange(total, dtype=jnp.int32)
-    station_in = jnp.repeat(slot_station, 2)
+    by_chan = slot_station.reshape(n_chan, -1)
+    arrived = jnp.concatenate([by_chan[: n_chan // 2], by_chan[n_chan // 2 :][::-1]]).reshape(-1)
+    station_in = jnp.repeat(arrived, 2)
     place = (station_in[None, :] == index[:, None] // 2) & (index[None, :] % 2 == index[:, None] % 2)
     place = place.astype(jnp.bfloat16)
     rows = jnp.asarray(sort_rows(n_time, parts))
     lanes = jnp.asarray(sort_lanes(128 // inputs, inputs))
-    pieces = [gather(got, rows, lanes, place, n_chan, n_time, parts, inputs) for got in (got_late, got_early)]
-    return correlate(pieces, pair_blocks, 1.0 / (n_time * frame_count))
+    pieces = [
+        gather(got, rows, lanes, place, n_chan, n_time, parts, limit)
+        for got, limit in ((got_late, LIMIT_A), (got_early, LIMIT_B))
+    ]
+    upper = lax.axis_index("chan") >= n_chan // 2
+    return correlate(pieces, pair_blocks, upper, 1.0 / (n_time * frame_count))
 
 
 def solution(mesh):

time: 156 us -> 151 us (0.968)
  Pallas kernels: 40.3 us -> 37 us
  starting transfers between devices: 27.5 us -> 25.8 us
    pallas_call x2, Pallas kernels: 27.2 us -> 22.2 us  [front(): pl.pallas_call(functools.partial(front_kernel, inputs, channels, segments...]
    all_to_all x2, starting transfers between devices: 23.9 us -> 22.2 us  [turn(): lax.all_to_all(pieces, OWNERS, split_axis=0, concat_axis=0, tiled=True, a...]
    pallas_call x2, Pallas kernels: 7.59 us -> 9.25 us  [gather(): pl.pallas_call(functools.partial(gather_kernel, n_chan), out_shape=jax.Sh...]
  transfers between devices with their start and end apart: 4 -> 4, of which waited for: 3 -> 3; matrix products, arithmetic and copies ran while one was open for 2% -> 3% of each run, Pallas kernels for 11% -> 12%
where the time goes in v3:
time: 151 us; the launch traced here: 150 us
  waiting for transfers between devices  81.2 us (54%)
  Pallas kernels  37 us (25%)
  starting transfers between devices  25.8 us (17%)
  local copies, waits for them, and re-layouts  5.16 us (3%)
    all_to_all x2, waiting for transfers between devices, turn(): lax.all_to_all(pieces, OWNERS, split_axis=0, concat_axis=0, tiled=True, a...  60.6 us
    pallas_call x2, Pallas kernels, front(): pl.pallas_call(functools.partial(front_kernel, inputs, channels, segments...  22.2 us
    all_to_all x2, starting transfers between devices, turn(): lax.all_to_all(pieces, OWNERS, split_axis=0, concat_axis=0, tiled=True, a...  22.2 us
    ppermute x1, waiting for transfers between devices, local(): lax.ppermute(head, 'tm', [(i, (i - 1) % n_time) for i in range(n_time)])  20.6 us
    pallas_call x2, Pallas kernels, gather(): pl.pallas_call(functools.partial(gather_kernel, n_chan), out_shape=jax.Sh...  9.25 us
    pallas_call x1, Pallas kernels, correlate(): pl.pallas_call(functools.partial(correlate_kernel, scale), out_shape=jax....  5.58 us
    ppermute x1, starting transfers between devices, local(): before = lax.ppermute(tail, 'tm', [(i, i + 1) for i in range(n_time - 1)])  3.54 us
  transfers between devices with their start and end apart: 4, of which 3 were waited for; matrix products, arithmetic and copies ran while one was open for 3% of the time, Pallas kernels for 12%

profile of v3, /device:TPU:1, one launch (start us, length us, event | category | flops | bytes accessed | tf_op | source)
XLA Modules:
  0.0 150.4 jit_solution(5497600859511876147)
XLA Ops:
  0.0 10.8 %front.2 = bf16[2048,512]{1,0:T(8,128)(2,1)} custom-call(f32[1]{0:T(128)} %bitcast.1.refs_0_, bf16[2,32,32768]{2,1,0:T(8,128)(2,1)} %refs_2_.2, f32[16,1024]{1,0:T(8,128)} %refs_4_.1, bf16[1056,1024]{1,0:T(8,128)(2,1)} %constant.55.clone.refs_3_.refs_5_), custom_call_target="tpu_custom_call" | custom-call | flops 2147483648 | bytes 16777216 | tf_op jit(solution)/shard_map/front/pallas_call | solution.py:160
  10.8 16.7 %all-to-all-start = ((bf16[256,8,512]{2,1,0:T(8,128)(2,1)}), bf16[256,8,512]{2,1,0:T(8,128)(2,1)}, u32[]{:S(2)}, u32[]{:S(2)}) async-start(bf16[256,8,512]{2,1,0:T(8,128)(2,1)} %bitcast.8), calls=%async_computation | async-start | bytes 4194304 | tf_op jit(solution)/shard_map/all_to_all | solution.py:320
  27.5 1.3 slice.38
  28.8 3.5 %collective-permute-start = (bf16[2,32,8192]{2,1,0:T(8,128)(2,1)S(1)}, bf16[2,32,8192]{2,1,0:T(8,128)(2,1)S(1)}, u32[]{:S(2)}, u32[]{:S(2)}) collective-permute-start(bf16[2,32,8192]{2,1,0:T(8,128)(2,1)S(1)} %slice.38), channel_id=1, source_target_pairs={{0,16},{16,32},{32,48},{48,64},{64,80},{80,96},{96,112},{112,128},... | collective-permute-start | bytes 3145736 | tf_op jit(solution)/shard_map/ppermute | solution.py:331
  32.3 1.2 slice.39
  33.6 0.1 collective-permute-start.1
  33.7 20.6 %collective-permute-done.1.refs_3_ = bf16[2,32,7168]{2,1,0:T(8,128)(2,1)S(1)} collective-permute-done((bf16[2,32,7168]{2,1,0:T(8,128)(2,1)S(1)}, bf16[2,32,7168]{2,1,0:T(8,128)(2,1)S(1)}, u32[]{:S(2)}, u32[]{:S(2)}) %collective-permute-start.1) | collective-permute-done | bytes 917536 | tf_op jit(solution)/shard_map/ppermute | solution.py:332
  54.3 0.0 copy-start.5
  54.3 0.0 collective-permute-done.refs_1_
  54.3 1.0 copy-done.5
  55.3 0.0 copy-start.4
  55.3 1.0 copy-done.4
  56.2 11.4 %front.3 = bf16[2048,512]{1,0:T(8,128)(2,1)} custom-call(f32[1]{0:T(128)} %bitcast.1.refs_0_, bf16[2,32,8192]{2,1,0:T(8,128)(2,1)} %copy-done.4, bf16[2,32,32768]{2,1,0:T(8,128)(2,1)} %refs_2_.2, bf16[2,32,7168]{2,1,0:T(8,128)(2,1)} %copy-done.5, f32[16,1024]{1,0:T(8,128)} %refs_4_.1, bf16[1056,1024]{1,0:T(8,128)(2,1)} %constant.55.clone.refs_3_.refs_5_), custom_call_target="tpu_custom_call" | custom-call | flops 2147483648 | bytes 16777216 | tf_op jit(solution)/shard_map/front/pallas_call | solution.py:160
  67.6 13.9 %all-to-all-done = bf16[256,8,512]{2,1,0:T(8,128)(2,1)} async-done(((bf16[256,8,512]{2,1,0:T(8,128)(2,1)}), bf16[256,8,512]{2,1,0:T(8,128)(2,1)}, u32[]{:S(2)}, u32[]{:S(2)}) %all-to-all-start) | async-done | bytes 2097184 | tf_op jit(solution)/shard_map/all_to_all | solution.py:320
  81.5 0.0 copy-start.7
  81.5 0.0 copy-start.6
  81.5 5.5 %all-to-all-start.1 = ((bf16[256,8,512]{2,1,0:T(8,128)(2,1)}), bf16[256,8,512]{2,1,0:T(8,128)(2,1)S(1)}, u32[]{:S(2)}, u32[]{:S(2)}) async-start(bf16[256,8,512]{2,1,0:T(8,128)(2,1)} %bitcast.7), calls=%async_computation.1 | async-start | bytes 4194304 | tf_op jit(solution)/shard_map/all_to_all | solution.py:320
  87.0 0.0 copy-done.7
  87.0 0.1 slice.35
  87.1 0.1 slice.37
  87.2 0.1 reshape.123
  87.3 0.0 copy-done.6
  87.3 0.1 copy.9
  87.4 0.1 reshape.116
  87.4 0.1 broadcast_in_dim.2
  87.6 0.1 eq.32
  87.7 0.1 pad_add_fusion.1.scalars
  87.8 1.0 and_convert_fusion.place_ref
  88.8 0.0 copy-start.1
  88.8 0.0 copy-start.2
  88.8 0.0 copy-start.3
  88.8 6.2 %gather.2.refs_0_ = bf16[2,4,512,256]{3,2,1,0:T(8,128)(2,1)} custom-call(bf16[2048,512]{1,0:T(8,128)(2,1)} %bitcast.3.got, bf16[2,128,128]{2,1,0:T(8,128)(2,1)} %constant.56.clone.rows_ref, bf16[512,512]{1,0:T(8,128)(2,1)} %constant.57.clone.lanes_ref, bf16[512,512]{1,0:T(8,128)(2,1)} %and_convert_fusion.place_ref), custom_call_target="tpu_custom_call" | custom-call | flops 4000000000 | bytes 8388608 | tf_op jit(solution)/shard_map/gather/pallas_call | solution.py:241
  95.0 46.8 %all-to-all-done.1 = bf16[256,8,512]{2,1,0:T(8,128)(2,1)S(1)} async-done(((bf16[256,8,512]{2,1,0:T(8,128)(2,1)}), bf16[256,8,512]{2,1,0:T(8,128)(2,1)S(1)}, u32[]{:S(2)}, u32[]{:S(2)}) %all-to-all-start.1) | async-done | bytes 2097184 | tf_op jit(solution)/shard_map/all_to_all | solution.py:320
  141.8 0.0 copy-done.1
  141.8 0.0 copy-done.2
  141.8 0.0 copy-done.3
  141.8 0.0 copy-start
  141.8 3.0 %gather.3.refs_1_ = bf16[2,4,512,256]{3,2,1,0:T(8,128)(2,1)S(1)} custom-call(bf16[2048,512]{1,0:T(8,128)(2,1)S(1)} %bitcast.6, bf16[2,128,128]{2,1,0:T(8,128)(2,1)S(1)} %copy-done.3, bf16[512,512]{1,0:T(8,128)(2,1)S(1)} %copy-done.2, bf16[512,512]{1,0:T(8,128)(2,1)S(1)} %copy-done.1), custom_call_target="tpu_custom_call" | custom-call | flops 4000000000 | bytes 8388608 | tf_op jit(solution)/shard_map/gather/pallas_call | solution.py:241
  144.9 0.0 copy-done
  144.9 5.6 %correlate.1 = f32[4,10,2,128,128]{4,3,2,1,0:T(8,128)} custom-call(s32[21]{0:T(128)S(1)} %pad_add_fusion.1.scalars, bf16[2,4,512,256]{3,2,1,0:T(8,128)(2,1)S(1)} %copy-done, bf16[2,4,512,256]{3,2,1,0:T(8,128)(2,1)S(1)} %gather.3.refs_1_), custom_call_target="tpu_custom_call" | custom-call | tf_op jit(solution)/shard_map/correlate/pallas_call | solution.py:284
  (4 shorter events, 0.0 us)
Async XLA Ops:
  10.8 70.6 %all-to-all-start = ((bf16[256,8,512]{2,1,0:T(8,128)(2,1)}), bf16[256,8,512]{2,1,0:T(8,128)(2,1)}, u32[]{:S(2)}, u32[]{:S(2)}) async-start(bf16[256,8,512]{2,1,0:T(8,128)(2,1)} %bitcast.8), calls=%async_computation | async-start | bytes 4194304 | tf_op jit(solution)/shard_map/all_to_all | solution.py:320
  28.8 25.5 %collective-permute-start = (bf16[2,32,8192]{2,1,0:T(8,128)(2,1)S(1)}, bf16[2,32,8192]{2,1,0:T(8,128)(2,1)S(1)}, u32[]{:S(2)}, u32[]{:S(2)}) collective-permute-start(bf16[2,32,8192]{2,1,0:T(8,128)(2,1)S(1)} %slice.38), channel_id=1, source_target_pairs={{0,16},{16,32},{32,48},{48,64},{64,80},{80,96},{96,112},{112,128},... | collective-permute-start | bytes 3145736 | tf_op jit(solution)/shard_map/ppermute | solution.py:331
  33.6 20.7 %collective-permute-start.1 = (bf16[2,32,7168]{2,1,0:T(8,128)(2,1)S(1)}, bf16[2,32,7168]{2,1,0:T(8,128)(2,1)S(1)}, u32[]{:S(2)}, u32[]{:S(2)}) collective-permute-start(bf16[2,32,7168]{2,1,0:T(8,128)(2,1)S(1)} %slice.39), channel_id=1, source_target_pairs={{0,240},{16,0},{32,16},{48,32},{64,48},{80,64},{96,80},{112,96},{1... | collective-permute-start | bytes 2752520 | tf_op jit(solution)/shard_map/ppermute | solution.py:332
  54.3 1.0 copy-start.5
  55.3 1.0 copy-start.4
  81.5 5.5 %copy-start.7 = (s32[256]{0:T(256)S(1)}, s32[256]{0:T(256)}, u32[]{:S(2)}) copy-start(s32[256]{0:T(256)} %param.9) | copy-start | bytes 3076
  81.5 5.8 %copy-start.6 = (s32[10,2]{0,1:T(2,128)S(1)}, s32[10,2]{0,1:T(2,128)}, u32[]{:S(2)}) copy-start(s32[10,2]{0,1:T(2,128)} %param.10) | copy-start | bytes 244
  81.5 60.3 %all-to-all-start.1 = ((bf16[256,8,512]{2,1,0:T(8,128)(2,1)}), bf16[256,8,512]{2,1,0:T(8,128)(2,1)S(1)}, u32[]{:S(2)}, u32[]{:S(2)}) async-start(bf16[256,8,512]{2,1,0:T(8,128)(2,1)} %bitcast.7), calls=%async_computation.1 | async-start | bytes 4194304 | tf_op jit(solution)/shard_map/all_to_all | solution.py:320
  88.8 53.0 %copy-start.1 = (bf16[512,512]{1,0:T(8,128)(2,1)S(1)}, bf16[512,512]{1,0:T(8,128)(2,1)}, u32[]{:S(2)}) copy-start(bf16[512,512]{1,0:T(8,128)(2,1)} %and_convert_fusion.place_ref) | copy-start | bytes 1572868
  88.8 53.0 %copy-start.2 = (bf16[512,512]{1,0:T(8,128)(2,1)S(1)}, bf16[512,512]{1,0:T(8,128)(2,1)}, u32[]{:S(2)}) copy-start(bf16[512,512]{1,0:T(8,128)(2,1)} %constant.57.clone.lanes_ref) | copy-start | bytes 1572868
  88.8 53.0 %copy-start.3 = (bf16[2,128,128]{2,1,0:T(8,128)(2,1)S(1)}, bf16[2,128,128]{2,1,0:T(8,128)(2,1)}, u32[]{:S(2)}) copy-start(bf16[2,128,128]{2,1,0:T(8,128)(2,1)} %constant.56.clone.rows_ref) | copy-start | bytes 196612
  141.8 3.1 %copy-start = (bf16[2,4,512,256]{3,2,1,0:T(8,128)(2,1)S(1)}, bf16[2,4,512,256]{3,2,1,0:T(8,128)(2,1)}, u32[]{:S(2)}) copy-start(bf16[2,4,512,256]{3,2,1,0:T(8,128)(2,1)} %gather.2.refs_0_) | copy-start | bytes 6291460

commit v4 on v3

--- a/solution.py
+++ b/solution.py
@@ -258,43 +258,52 @@
 LIMIT_B = 20 * 2**20
 
 
-def correlate_kernel(scale, scalars, *refs):
-    pieces, out = refs[:-1], refs[-1]
-    for b in range(out.shape[1]):
-        sides = []
-        for end in range(2):
-            at = pl.ds(pl.multiple_of(scalars[2 * b + end] * TILE, TILE), TILE)
-            sides.append([jnp.concatenate([piece[0, 0, at, :], piece[1, 0, at, :]], 0) for piece in pieces])
-        gram = sum(
-            lax.dot_general(left, right, NT, preferred_element_type=jnp.float32)
-            for left, right in zip(*sides)
-        )
-        out[0, b, 0] = (gram[:TILE, :TILE] + gram[TILE:, TILE:]) * scale
-        out[0, b, 1] = (gram[TILE:, :TILE] - gram[:TILE, TILE:]) * scale
-
-
-def correlate(pieces, pair_blocks, upper, scale):
-    per_owner = pieces[0].shape[1]
+def correlate_kernel(first, scale, scalars, piece, *refs):
+    partial, (out_hbm, out, sems) = refs[0], refs[-3:]
+    per_owner, blocks = out.shape[:2]
+
+    def send(j):
+        channel = j
+        if not first:
+            channel = jnp.where(scalars[2 * blocks] > 0, (per_owner - j) % per_owner, j)
+        return pltpu.make_async_copy(out.at[j], out_hbm.at[channel], sems.at[j])
+
+    for j in range(per_owner):
+        for b in range(blocks):
+            sides = []
+            for end in range(2):
+                at = pl.ds(pl.multiple_of(scalars[2 * b + end] * TILE, TILE), TILE)
+                sides.append(jnp.concatenate([piece[0, j, at, :], piece[1, j, at, :]], 0))
+            gram = lax.dot_general(*sides, NT, preferred_element_type=jnp.float32)
+            real = gram[:TILE, :TILE] + gram[TILE:, TILE:]
+            imag = gram[TILE:, :TILE] - gram[:TILE, TILE:]
+            if first:
+                out[j, b, 0], out[j, b, 1] = real, imag
+            else:
+                out[j, b, 0] = (real + partial[j, b, 0]) * scale
+                out[j, b, 1] = (imag + partial[j, b, 1]) * scale
+        send(j).start()
+    for j in range(per_owner):
+        send(j).wait()
+
+
+def correlate(piece, partial, pair_blocks, upper, scale):
+    per_owner = piece.shape[1]
     blocks = pair_blocks.shape[0]
     scalars = jnp.concatenate([pair_blocks.reshape(-1), upper.astype(jnp.int32).reshape(1)])
-
-    def channel_of(j, scalars):
-        return jnp.where(scalars[2 * blocks] > 0, lax.rem(per_owner - j, per_owner), j)
-
+    shape = (per_owner, blocks, 2, TILE, TILE)
+    first = partial is None
+    operands = [piece] if first else [piece, partial]
     return pl.pallas_call(
-        functools.partial(correlate_kernel, scale),
-        out_shape=jax.ShapeDtypeStruct((per_owner, blocks, 2, TILE, TILE), jnp.float32),
-        grid_spec=pltpu.PrefetchScalarGridSpec(
-            num_scalar_prefetch=1,
-            grid=(per_owner,),
-            in_specs=[pl.BlockSpec((2, 1) + x.shape[2:], lambda j, scalars: (0, j, 0, 0)) for x in pieces],
-            out_specs=pl.BlockSpec(
-                (1, blocks, 2, TILE, TILE), lambda j, scalars: (channel_of(j, scalars), 0, 0, 0, 0)
-            ),
-        ),
+        functools.partial(correlate_kernel, first, scale),
+        out_shape=jax.ShapeDtypeStruct(shape, jnp.float32),
+        in_specs=[pl.BlockSpec(memory_space=pltpu.SMEM)] + [pl.BlockSpec(memory_space=pltpu.VMEM)] * len(operands),
+        out_specs=pl.BlockSpec(memory_space=pl.ANY),
+        scratch_shapes=[pltpu.VMEM(shape, jnp.float32), pltpu.SemaphoreType.DMA((per_owner,))],
         compiler_params=pltpu.CompilerParams(vmem_limit_bytes=LIMIT),
+        cost_estimate=pl.CostEstimate(flops=3 * 10**9, bytes_accessed=8 * 2**20, transcendentals=0),
         name="correlate",
-    )(scalars, *pieces)
+    )(scalars, *operands)
 
 
 def local(voltages, filter_taps, slot_station, pair_blocks):
@@ -346,12 +355,13 @@
     place = place.astype(jnp.bfloat16)
     rows = jnp.asarray(sort_rows(n_time, parts))
     lanes = jnp.asarray(sort_lanes(128 // inputs, inputs))
-    pieces = [
-        gather(got, rows, lanes, place, n_chan, n_time, parts, limit)
-        for got, limit in ((got_late, LIMIT_A), (got_early, LIMIT_B))
-    ]
     upper = lax.axis_index("chan") >= n_chan // 2
-    return correlate(pieces, pair_blocks, upper, 1.0 / (n_time * frame_count))
+    scale = 1.0 / (n_time * frame_count)
+    result = None
+    for got, limit in ((got_late, LIMIT_A), (got_early, LIMIT_B)):
+        piece = gather(got, rows, lanes, place, n_chan, n_time, parts, limit)
+        result = correlate(piece, result, pair_blocks, upper, scale)
+    return result
 
 
 def solution(mesh):

time: 151 us -> 149 us (0.987)
  waiting for transfers between devices: 81.2 us -> 74.2 us
  local copies, waits for them, and re-layouts: 5.16 us -> 9.1 us
    all_to_all x2, waiting for transfers between devices: 60.6 us -> 53.6 us  [turn(): lax.all_to_all(pieces, OWNERS, split_axis=0, concat_axis=0, tiled=True, a...]
    unnamed x17 -> x21, local copies, waits for them, and re-layouts: 2.04 us -> 5.99 us
    pallas_call x1 -> x2, Pallas kernels: 5.58 us -> 6.63 us  [correlate(): pl.pallas_call(functools.partial(correlate_kernel, first, scale), out_sha...]
  transfers between devices with their start and end apart: 4 -> 4, of which waited for: 3 -> 3; matrix products, arithmetic and copies ran while one was open for 3% -> 3% of each run, Pallas kernels for 12% -> 14%
where the time goes in v4:
time: 149 us
  waiting for transfers between devices  74.2 us (50%)
  Pallas kernels  37.9 us (25%)
  starting transfers between devices  25.8 us (17%)
  local copies, waits for them, and re-layouts  9.1 us (6%)
    all_to_all x2, waiting for transfers between devices, turn(): lax.all_to_all(pieces, OWNERS, split_axis=0, concat_axis=0, tiled=True, a...  53.6 us
    pallas_call x2, Pallas kernels, front(): pl.pallas_call(functools.partial(front_kernel, inputs, channels, segments...  22.2 us
    all_to_all x2, starting transfers between devices, turn(): lax.all_to_all(pieces, OWNERS, split_axis=0, concat_axis=0, tiled=True, a...  22.2 us
    ppermute x1, waiting for transfers between devices, local(): lax.ppermute(head, 'tm', [(i, (i - 1) % n_time) for i in range(n_time)])  20.6 us
    pallas_call x2, Pallas kernels, gather(): pl.pallas_call(functools.partial(gather_kernel, n_chan), out_shape=jax.Sh...  9.16 us
    pallas_call x2, Pallas kernels, correlate(): pl.pallas_call(functools.partial(correlate_kernel, first, scale), out_sha...  6.63 us
    unnamed x21, local copies, waits for them, and re-layouts  5.99 us
    ppermute x1, starting transfers between devices, local(): before = lax.ppermute(tail, 'tm', [(i, i + 1) for i in range(n_time - 1)])  3.54 us
  transfers between devices with their start and end apart: 4, of which 3 were waited for; matrix products, arithmetic and copies ran while one was open for 3% of the time, Pallas kernels for 14%

profile of v4, /device:TPU:1, one launch (start us, length us, event | category | flops | bytes accessed | tf_op | source)
XLA Modules:
  0.0 148.5 jit_solution(13445903405166314744)
XLA Ops:
  0.0 10.8 %front.2 = bf16[2048,512]{1,0:T(8,128)(2,1)} custom-call(f32[1]{0:T(128)} %bitcast.1.refs_0_, bf16[2,32,32768]{2,1,0:T(8,128)(2,1)} %refs_2_.2, f32[16,1024]{1,0:T(8,128)} %refs_4_.1, bf16[1056,1024]{1,0:T(8,128)(2,1)} %constant.55.clone.refs_3_.refs_5_), custom_call_target="tpu_custom_call" | custom-call | flops 2147483648 | bytes 16777216 | tf_op jit(solution)/shard_map/front/pallas_call | solution.py:160
  10.8 16.7 %all-to-all-start.1 = ((bf16[256,8,512]{2,1,0:T(8,128)(2,1)}), bf16[256,8,512]{2,1,0:T(8,128)(2,1)}, u32[]{:S(2)}, u32[]{:S(2)}) async-start(bf16[256,8,512]{2,1,0:T(8,128)(2,1)} %bitcast.8), calls=%async_computation.1 | async-start | bytes 4194304 | tf_op jit(solution)/shard_map/all_to_all | solution.py:329
  27.5 1.3 slice.34
  28.8 3.5 %collective-permute-start = (bf16[2,32,8192]{2,1,0:T(8,128)(2,1)S(1)}, bf16[2,32,8192]{2,1,0:T(8,128)(2,1)S(1)}, u32[]{:S(2)}, u32[]{:S(2)}) collective-permute-start(bf16[2,32,8192]{2,1,0:T(8,128)(2,1)S(1)} %slice.34), channel_id=1, source_target_pairs={{0,16},{16,32},{32,48},{48,64},{64,80},{80,96},{96,112},{112,128},... | collective-permute-start | bytes 3145736 | tf_op jit(solution)/shard_map/ppermute | solution.py:340
  32.3 1.2 slice.35
  33.6 0.1 collective-permute-start.1
  33.7 20.6 %collective-permute-done.1.refs_3_ = bf16[2,32,7168]{2,1,0:T(8,128)(2,1)S(1)} collective-permute-done((bf16[2,32,7168]{2,1,0:T(8,128)(2,1)S(1)}, bf16[2,32,7168]{2,1,0:T(8,128)(2,1)S(1)}, u32[]{:S(2)}, u32[]{:S(2)}) %collective-permute-start.1) | collective-permute-done | bytes 917536 | tf_op jit(solution)/shard_map/ppermute | solution.py:341
  54.3 0.0 copy-start.7
  54.3 0.0 collective-permute-done.refs_1_
  54.3 0.9 copy-done.7
  55.3 0.0 copy-start.6
  55.3 1.0 copy-done.6
  56.2 11.3 %front.3 = bf16[2048,512]{1,0:T(8,128)(2,1)} custom-call(f32[1]{0:T(128)} %bitcast.1.refs_0_, bf16[2,32,8192]{2,1,0:T(8,128)(2,1)} %copy-done.6, bf16[2,32,32768]{2,1,0:T(8,128)(2,1)} %refs_2_.2, bf16[2,32,7168]{2,1,0:T(8,128)(2,1)} %copy-done.7, f32[16,1024]{1,0:T(8,128)} %refs_4_.1, bf16[1056,1024]{1,0:T(8,128)(2,1)} %constant.55.clone.refs_3_.refs_5_), custom_call_target="tpu_custom_call" | custom-call | flops 2147483648 | bytes 16777216 | tf_op jit(solution)/shard_map/front/pallas_call | solution.py:160
  67.6 13.9 %all-to-all-done.1 = bf16[256,8,512]{2,1,0:T(8,128)(2,1)} async-done(((bf16[256,8,512]{2,1,0:T(8,128)(2,1)}), bf16[256,8,512]{2,1,0:T(8,128)(2,1)}, u32[]{:S(2)}, u32[]{:S(2)}) %all-to-all-start.1) | async-done | bytes 2097184 | tf_op jit(solution)/shard_map/all_to_all | solution.py:329
  81.5 0.0 copy-start.9
  81.5 0.0 copy-start.8
  81.5 5.5 %all-to-all-start = ((bf16[256,8,512]{2,1,0:T(8,128)(2,1)}), bf16[256,8,512]{2,1,0:T(8,128)(2,1)S(1)}, u32[]{:S(2)}, u32[]{:S(2)}) async-start(bf16[256,8,512]{2,1,0:T(8,128)(2,1)} %bitcast.7), calls=%async_computation | async-start | bytes 4194304 | tf_op jit(solution)/shard_map/all_to_all | solution.py:329
  87.0 0.0 copy-done.9
  87.0 0.1 slice.37
  87.1 0.1 slice.39
  87.2 0.1 reshape.125
  87.3 0.0 copy-done.8
  87.3 0.1 copy.9
  87.4 0.1 reshape.118
  87.4 0.1 broadcast_in_dim.2
  87.6 0.1 eq.32
  87.7 0.1 pad_add_fusion.1.scalars
  87.8 1.0 and_convert_fusion.place_ref
  88.8 6.1 %gather.3.piece = bf16[2,4,512,256]{3,2,1,0:T(8,128)(2,1)} custom-call(bf16[2048,512]{1,0:T(8,128)(2,1)} %bitcast.5.got, bf16[2,128,128]{2,1,0:T(8,128)(2,1)} %constant.56.clone.rows_ref, bf16[512,512]{1,0:T(8,128)(2,1)} %constant.57.clone.lanes_ref, bf16[512,512]{1,0:T(8,128)(2,1)} %and_convert_fusion.place_ref), custom_call_target="tpu_custom_call" | custom-call | flops 4000000000 | bytes 8388608 | tf_op jit(solution)/shard_map/gather/pallas_call | solution.py:241
  94.9 0.0 copy-start.5
  94.9 1.6 %copy-done.5 = bf16[2,4,512,256]{3,2,1,0:T(8,128)(2,1)S(1)} copy-done((bf16[2,4,512,256]{3,2,1,0:T(8,128)(2,1)S(1)}, bf16[2,4,512,256]{3,2,1,0:T(8,128)(2,1)}, u32[]{:S(2)}) %copy-start.5) | copy-done | bytes 2097176
  96.5 0.0 copy-start.2
  96.5 0.0 copy-start.3
  96.5 0.0 copy-start.4
  96.5 3.2 %correlate.2.refs_0_ = f32[4,10,2,128,128]{4,3,2,1,0:T(8,128)S(1)} custom-call(s32[21]{0:T(128)S(1)} %pad_add_fusion.1.scalars, bf16[2,4,512,256]{3,2,1,0:T(8,128)(2,1)S(1)} %copy-done.5), custom_call_target="tpu_custom_call" | custom-call | flops 3000000000 | bytes 8388608 | tf_op jit(solution)/shard_map/correlate/pallas_call | solution.py:297
  99.7 0.0 copy-start
  99.7 2.3 %copy-done = f32[4,10,2,128,128]{4,3,2,1,0:T(8,128)} copy-done((f32[4,10,2,128,128]{4,3,2,1,0:T(8,128)}, f32[4,10,2,128,128]{4,3,2,1,0:T(8,128)S(1)}, u32[]{:S(2)}) %copy-start) | copy-done | bytes 5242904
  102.0 39.7 %all-to-all-done = bf16[256,8,512]{2,1,0:T(8,128)(2,1)S(1)} async-done(((bf16[256,8,512]{2,1,0:T(8,128)(2,1)}), bf16[256,8,512]{2,1,0:T(8,128)(2,1)S(1)}, u32[]{:S(2)}, u32[]{:S(2)}) %all-to-all-start) | async-done | bytes 2097184 | tf_op jit(solution)/shard_map/all_to_all | solution.py:329
  141.8 0.0 copy-done.2
  141.8 0.0 copy-done.3
  141.8 0.0 copy-done.4
  141.8 0.0 copy-start.1
  141.8 3.0 %gather.2.piece = bf16[2,4,512,256]{3,2,1,0:T(8,128)(2,1)S(1)} custom-call(bf16[2048,512]{1,0:T(8,128)(2,1)S(1)} %bitcast.6, bf16[2,128,128]{2,1,0:T(8,128)(2,1)S(1)} %copy-done.4, bf16[512,512]{1,0:T(8,128)(2,1)S(1)} %copy-done.3, bf16[512,512]{1,0:T(8,128)(2,1)S(1)} %copy-done.2), custom_call_target="tpu_custom_call" | custom-call | flops 4000000000 | bytes 8388608 | tf_op jit(solution)/shard_map/gather/pallas_call | solution.py:241
  144.9 0.0 copy-done.1
  144.9 3.5 %correlate.3 = f32[4,10,2,128,128]{4,3,2,1,0:T(8,128)} custom-call(s32[21]{0:T(128)S(1)} %pad_add_fusion.1.scalars, bf16[2,4,512,256]{3,2,1,0:T(8,128)(2,1)S(1)} %gather.2.piece, f32[4,10,2,128,128]{4,3,2,1,0:T(8,128)S(1)} %copy-done.1), custom_call_target="tpu_custom_call" | custom-call | flops 3000000000 | bytes 8388608 | tf_op jit(solution)/shard_map/correlate/pallas_call | solution.py:297
  (4 shorter events, 0.0 us)
Async XLA Ops:
  10.8 70.6 %all-to-all-start.1 = ((bf16[256,8,512]{2,1,0:T(8,128)(2,1)}), bf16[256,8,512]{2,1,0:T(8,128)(2,1)}, u32[]{:S(2)}, u32[]{:S(2)}) async-start(bf16[256,8,512]{2,1,0:T(8,128)(2,1)} %bitcast.8), calls=%async_computation.1 | async-start | bytes 4194304 | tf_op jit(solution)/shard_map/all_to_all | solution.py:329
  28.8 25.5 %collective-permute-start = (bf16[2,32,8192]{2,1,0:T(8,128)(2,1)S(1)}, bf16[2,32,8192]{2,1,0:T(8,128)(2,1)S(1)}, u32[]{:S(2)}, u32[]{:S(2)}) collective-permute-start(bf16[2,32,8192]{2,1,0:T(8,128)(2,1)S(1)} %slice.34), channel_id=1, source_target_pairs={{0,16},{16,32},{32,48},{48,64},{64,80},{80,96},{96,112},{112,128},... | collective-permute-start | bytes 3145736 | tf_op jit(solution)/shard_map/ppermute | solution.py:340
  33.6 20.7 %collective-permute-start.1 = (bf16[2,32,7168]{2,1,0:T(8,128)(2,1)S(1)}, bf16[2,32,7168]{2,1,0:T(8,128)(2,1)S(1)}, u32[]{:S(2)}, u32[]{:S(2)}) collective-permute-start(bf16[2,32,7168]{2,1,0:T(8,128)(2,1)S(1)} %slice.35), channel_id=1, source_target_pairs={{0,240},{16,0},{32,16},{48,32},{64,48},{80,64},{96,80},{112,96},{1... | collective-permute-start | bytes 2752520 | tf_op jit(solution)/shard_map/ppermute | solution.py:341
  54.3 0.9 copy-start.7
  55.3 1.0 copy-start.6
  81.5 5.5 %copy-start.9 = (s32[256]{0:T(256)S(1)}, s32[256]{0:T(256)}, u32[]{:S(2)}) copy-start(s32[256]{0:T(256)} %param.9) | copy-start | bytes 3076
  81.5 5.8 %copy-start.8 = (s32[10,2]{0,1:T(2,128)S(1)}, s32[10,2]{0,1:T(2,128)}, u32[]{:S(2)}) copy-start(s32[10,2]{0,1:T(2,128)} %param.10) | copy-start | bytes 244
  81.5 60.3 %all-to-all-start = ((bf16[256,8,512]{2,1,0:T(8,128)(2,1)}), bf16[256,8,512]{2,1,0:T(8,128)(2,1)S(1)}, u32[]{:S(2)}, u32[]{:S(2)}) async-start(bf16[256,8,512]{2,1,0:T(8,128)(2,1)} %bitcast.7), calls=%async_computation | async-start | bytes 4194304 | tf_op jit(solution)/shard_map/all_to_all | solution.py:329
  94.9 1.6 %copy-start.5 = (bf16[2,4,512,256]{3,2,1,0:T(8,128)(2,1)S(1)}, bf16[2,4,512,256]{3,2,1,0:T(8,128)(2,1)}, u32[]{:S(2)}) copy-start(bf16[2,4,512,256]{3,2,1,0:T(8,128)(2,1)} %gather.3.piece) | copy-start | bytes 6291460
  96.5 45.3 %copy-start.2 = (bf16[512,512]{1,0:T(8,128)(2,1)S(1)}, bf16[512,512]{1,0:T(8,128)(2,1)}, u32[]{:S(2)}) copy-start(bf16[512,512]{1,0:T(8,128)(2,1)} %and_convert_fusion.place_ref) | copy-start | bytes 1572868
  96.5 45.3 %copy-start.3 = (bf16[512,512]{1,0:T(8,128)(2,1)S(1)}, bf16[512,512]{1,0:T(8,128)(2,1)}, u32[]{:S(2)}) copy-start(bf16[512,512]{1,0:T(8,128)(2,1)} %constant.57.clone.lanes_ref) | copy-start | bytes 1572868
  96.5 45.3 %copy-start.4 = (bf16[2,128,128]{2,1,0:T(8,128)(2,1)S(1)}, bf16[2,128,128]{2,1,0:T(8,128)(2,1)}, u32[]{:S(2)}) copy-start(bf16[2,128,128]{2,1,0:T(8,128)(2,1)} %constant.56.clone.rows_ref) | copy-start | bytes 196612
  99.7 2.4 %copy-start = (f32[4,10,2,128,128]{4,3,2,1,0:T(8,128)}, f32[4,10,2,128,128]{4,3,2,1,0:T(8,128)S(1)}, u32[]{:S(2)}) copy-start(f32[4,10,2,128,128]{4,3,2,1,0:T(8,128)S(1)} %correlate.2.refs_0_) | copy-start | bytes 15728644
  141.8 3.1 %copy-start.1 = (f32[4,10,2,128,128]{4,3,2,1,0:T(8,128)S(1)}, f32[4,10,2,128,128]{4,3,2,1,0:T(8,128)}, u32[]{:S(2)}) copy-start(f32[4,10,2,128,128]{4,3,2,1,0:T(8,128)} %copy-done) | copy-start | bytes 15728644
